TPU v7x, 256 devices: a whole 4x4x8 slice. The times are simulated.
256 devices in a mesh: rep: 16 (over y, x_lo, core), gz: 16 (over z, x_hi).
Axes of the slice: x: 4 (x_hi: 2, x_lo: 2; x = x_hi * 2 + x_lo), y: 4, z: 8, core: 2. Of those that a mesh axis runs over, the one named last changes fastest.
Arguments:
- field: float32 [16, 64, 256, 256], P('rep', 'gz'), may hold values from -4 to 4
- momenta: float32 [16, 64, 256, 256], P('rep', 'gz'), may hold values from -6 to 6
- counts: int32 [16], replicated, may hold values from 0 to 9, as said below
- accept: int32 [16], P('rep'), may hold values 0 or 1
Outputs:
- new_field: float32 [16, 64, 256, 256], P('rep', 'gz')
Inputs may be any that keep to these rules, and one draw needn't show every extreme that they name: counts sum to 16; exactly one replica has the largest count, 9; every other count is 0 or 1.
All inputs are finite; a program needn't handle non-finite values. No bound on the sum of `accept` on one device may be relied on, other than what follows from the above.
Results may differ from a plain program's by a relative error of at most 0.0003.
Values sent between devices are 32-bit elements; how exact they have to be, the bound alone decides.
A program may use at most 64 MiB of HBM per device.

v0:
```python
import jax
import jax.numpy as jnp
from jax import lax
from jax.sharding import PartitionSpec as P

STEPS = 4


KAPPA = 0.16
LAMBDA = 0.015
EPS = 0.75


def padded_2(cells, sides, width):
    for axis, dim in sides:
        count = lax.axis_size(axis)
        head = lax.slice_in_dim(cells, 0, width, axis=dim)
        tail = lax.slice_in_dim(cells, cells.shape[dim] - width, cells.shape[dim], axis=dim)
        cells = jnp.concatenate(
            [
                lax.ppermute(tail, axis, [(i, (i + 1) % count) for i in range(count)]),
                cells,
                lax.ppermute(head, axis, [((i + 1) % count, i) for i in range(count)]),
            ],
            axis=dim,
        )
    return cells


def parent_table(counts):
    cum = jnp.cumsum(counts)
    slots = jnp.arange(counts.shape[0], dtype=jnp.int32)
    return jnp.sum((cum[None, :] <= slots[:, None]).astype(jnp.int32), axis=1)


def force(phi):
    padded = padded_2(phi, (("gz", 0),), 1)
    beside_all = padded[2:] + padded[:-2]
    beside_all = beside_all + jnp.roll(phi, 1, 1) + jnp.roll(phi, -1, 1)
    beside_all = beside_all + jnp.roll(phi, 1, 2) + jnp.roll(phi, -1, 2)
    return 2.0 * KAPPA * beside_all - 2.0 * phi - 4.0 * LAMBDA * phi * (phi * phi - 1.0)


def local(field, momenta, counts, accept):
    parents = parent_table(counts)
    mine = lax.axis_index("rep")
    target = parents[mine]
    piece = lax.all_gather(field, "rep", axis=0, tiled=True)
    rows = jnp.arange(piece.shape[0], dtype=jnp.int32)
    weight = (rows == target).astype(jnp.float32)
    start = jnp.sum(weight[:, None, None, None] * piece, axis=0, keepdims=True)
    phi = start[0]
    mom = momenta[0] + 0.5 * EPS * force(phi)
    for step in range(STEPS):
        phi = phi + EPS * mom
        if step < STEPS - 1:
            mom = mom + EPS * force(phi)
    return jnp.where(accept[0] == 1, phi, start[0])[None]


def solution(mesh):
    placed = (P("rep", "gz", None, None), P("rep", "gz", None, None), P(), P("rep"))
    return jax.shard_map(
        local, mesh=mesh, in_specs=placed, out_specs=P("rep", "gz", None, None), check_vma=False
    )
```

profile of v0, /device:TPU:1, one launch (start us, length us, event | category | flops | bytes accessed | tf_op | source)
XLA Modules:
  0.0 193.3 jit_solution(11569639268715830877)
XLA Ops:
  6.5 0.7 all-gather.2.cloned.1.call-update
  7.3 0.7 copy.8
  8.9 0.6 dynamic_slice.3
  9.5 0.6 compare_convert_fusion
  10.2 97.5 %all-gather.2.cloned.1.call-done = f32[16,4,256,256]{3,2,1,0:T(8,128)} async-done(((f32[1,4,256,256]{3,2,1,0:T(8,128)}), f32[16,4,256,256]{3,2,1,0:T(8,128)}) %all-gather.2.cloned.1.call-update) | async-done | bytes 16777232 | tf_op jit(solution)/shard_map/all_gather | solution.py:48
  107.6 7.4 %multiply_reduce_fusion = f32[4,256,256]{2,1,0:T(8,128)S(1)} fusion(f32[16,4,256,256]{3,2,1,0:T(8,128)} %all-gather.2.cloned.1.call-done, f32[16]{0:T(128)S(1)} %compare_convert_fusion), kind=kLoop, calls=%fused_computation | loop fusion | flops 8126464 | bytes 17825856 | tf_op jit(solution)/shard_map/reduce_sum | solution.py:51
  115.6 5.5 %collective-permute-start = (f32[1,256,256]{2,1,0:T(8,128)S(1)}, f32[1,256,256]{2,1,0:T(8,128)S(1)}, u32[]{:S(2)}, u32[]{:S(2)}) collective-permute-start(f32[1,256,256]{2,1,0:T(8,128)S(1)} %get-tuple-element.41), channel_id=1, source_target_pairs={{1,0},{2,1},{3,2},{4,3},{5,4},{6,5},{7,6},{8,7},{9,8},{10,9},{11,1... | collective-permute-start | bytes 786440 | tf_op jit(solution)/shard_map/ppermute | solution.py:23
  121.3 5.3 %collective-permute-done = f32[1,256,256]{2,1,0:T(8,128)S(1)} collective-permute-done((f32[1,256,256]{2,1,0:T(8,128)S(1)}, f32[1,256,256]{2,1,0:T(8,128)S(1)}, u32[]{:S(2)}, u32[]{:S(2)}) %collective-permute-start) | collective-permute-done | bytes 262176 | tf_op jit(solution)/shard_map/ppermute | solution.py:23
  126.6 5.5 %collective-permute-done.1 = f32[1,256,256]{2,1,0:T(8,128)S(1)} collective-permute-done((f32[1,256,256]{2,1,0:T(8,128)S(1)}, f32[1,256,256]{2,1,0:T(8,128)S(1)}, u32[]{:S(2)}, u32[]{:S(2)}) %collective-permute-start.1) | collective-permute-done | bytes 262176 | tf_op jit(solution)/shard_map/ppermute | solution.py:21
  132.1 1.0 multiply_add_fusion.2
  133.2 0.4 fusion.61
  133.6 4.7 %collective-permute-start.2 = (f32[1,256,256]{2,1,0:T(8,128)S(1)}, f32[1,256,256]{2,1,0:T(8,128)S(1)}, u32[]{:S(2)}, u32[]{:S(2)}) collective-permute-start(f32[1,256,256]{2,1,0:T(8,128)S(1)} %get-tuple-element.31), channel_id=1, source_target_pairs={{1,0},{2,1},{3,2},{4,3},{5,4},{6,5},{7,6},{8,7},{9,8},{10,9},{11,1... | collective-permute-start | bytes 786440 | tf_op jit(solution)/shard_map/ppermute | solution.py:23
  138.6 4.4 %collective-permute-done.2 = f32[1,256,256]{2,1,0:T(8,128)S(1)} collective-permute-done((f32[1,256,256]{2,1,0:T(8,128)S(1)}, f32[1,256,256]{2,1,0:T(8,128)S(1)}, u32[]{:S(2)}, u32[]{:S(2)}) %collective-permute-start.2) | collective-permute-done | bytes 262176 | tf_op jit(solution)/shard_map/ppermute | solution.py:23
  142.9 5.9 %collective-permute-done.3 = f32[1,256,256]{2,1,0:T(8,128)S(1)} collective-permute-done((f32[1,256,256]{2,1,0:T(8,128)S(1)}, f32[1,256,256]{2,1,0:T(8,128)S(1)}, u32[]{:S(2)}, u32[]{:S(2)}) %collective-permute-start.3) | collective-permute-done | bytes 262176 | tf_op jit(solution)/shard_map/ppermute | solution.py:21
  148.8 0.9 multiply_add_fusion.1
  149.9 0.4 fusion.56
  150.3 5.4 %collective-permute-start.4 = (f32[1,256,256]{2,1,0:T(8,128)S(1)}, f32[1,256,256]{2,1,0:T(8,128)S(1)}, u32[]{:S(2)}, u32[]{:S(2)}) collective-permute-start(f32[1,256,256]{2,1,0:T(8,128)S(1)} %get-tuple-element.21), channel_id=1, source_target_pairs={{1,0},{2,1},{3,2},{4,3},{5,4},{6,5},{7,6},{8,7},{9,8},{10,9},{11,1... | collective-permute-start | bytes 786440 | tf_op jit(solution)/shard_map/ppermute | solution.py:23
  155.9 4.1 %collective-permute-done.4 = f32[1,256,256]{2,1,0:T(8,128)S(1)} collective-permute-done((f32[1,256,256]{2,1,0:T(8,128)S(1)}, f32[1,256,256]{2,1,0:T(8,128)S(1)}, u32[]{:S(2)}, u32[]{:S(2)}) %collective-permute-start.4) | collective-permute-done | bytes 262176 | tf_op jit(solution)/shard_map/ppermute | solution.py:23
  160.0 6.6 %collective-permute-done.5 = f32[1,256,256]{2,1,0:T(8,128)S(1)} collective-permute-done((f32[1,256,256]{2,1,0:T(8,128)S(1)}, f32[1,256,256]{2,1,0:T(8,128)S(1)}, u32[]{:S(2)}, u32[]{:S(2)}) %collective-permute-start.5) | collective-permute-done | bytes 262176 | tf_op jit(solution)/shard_map/ppermute | solution.py:21
  166.6 0.9 multiply_add_fusion
  168.1 5.5 %collective-permute-start.6 = (f32[1,256,256]{2,1,0:T(8,128)S(1)}, f32[1,256,256]{2,1,0:T(8,128)S(1)}, u32[]{:S(2)}, u32[]{:S(2)}) collective-permute-start(f32[1,256,256]{2,1,0:T(8,128)S(1)} %get-tuple-element.19), channel_id=1, source_target_pairs={{1,0},{2,1},{3,2},{4,3},{5,4},{6,5},{7,6},{8,7},{9,8},{10,9},{11,1... | collective-permute-start | bytes 786440 | tf_op jit(solution)/shard_map/ppermute | solution.py:23
  173.8 4.4 %collective-permute-done.6 = f32[1,256,256]{2,1,0:T(8,128)S(1)} collective-permute-done((f32[1,256,256]{2,1,0:T(8,128)S(1)}, f32[1,256,256]{2,1,0:T(8,128)S(1)}, u32[]{:S(2)}, u32[]{:S(2)}) %collective-permute-start.6) | collective-permute-done | bytes 262176 | tf_op jit(solution)/shard_map/ppermute | solution.py:23
  178.2 6.3 %collective-permute-done.7 = f32[1,256,256]{2,1,0:T(8,128)S(1)} collective-permute-done((f32[1,256,256]{2,1,0:T(8,128)S(1)}, f32[1,256,256]{2,1,0:T(8,128)S(1)}, u32[]{:S(2)}, u32[]{:S(2)}) %collective-permute-start.7) | collective-permute-done | bytes 262176 | tf_op jit(solution)/shard_map/ppermute | solution.py:21
  184.4 2.0 %fusion.13 = f32[1,4,256,256]{3,2,1,0:T(8,128)} fusion(f32[4,256,256]{2,1,0:T(8,128)S(1)} %multiply_reduce_fusion, f32[4,256,256]{2,1,0:T(8,128)S(1)} %get-tuple-element.5, f32[4,256,256]{2,1,0:T(8,128)S(1)} %get-tuple-element.6, f32[1,256,256]{2,1,0:T(8,128)S(1)} %collective-permute-done.7, f32[1,256,256]{2,1,0:T(8,128)S(1)} %collective-permute-done.6, ...), kind=kLoop, calls=%fused_computation.15 | loop fusion | flops 6291456 | bytes 8912897 | tf_op jit(solution)/shard_map/broadcast_in_dim | solution.py:58
  (28 shorter events, 2.7 us)
Async XLA Ops:
  6.5 125.5 %copy-start = (f32[1,4,256,256]{3,2,1,0:T(8,128)S(1)}, f32[1,4,256,256]{3,2,1,0:T(8,128)}, u32[]{:S(2)}) copy-start(f32[1,4,256,256]{3,2,1,0:T(8,128)} %param.5) | copy-start | bytes 3145732
  6.5 101.1 %all-gather.2.cloned.1.call-start = ((), (), s32[]{:S(2)}) async-start(), calls=%async_computation | async-start | bytes 17825792 | tf_op jit(solution)/shard_map/all_gather | solution.py:48
  115.6 11.0 %collective-permute-start = (f32[1,256,256]{2,1,0:T(8,128)S(1)}, f32[1,256,256]{2,1,0:T(8,128)S(1)}, u32[]{:S(2)}, u32[]{:S(2)}) collective-permute-start(f32[1,256,256]{2,1,0:T(8,128)S(1)} %get-tuple-element.41), channel_id=1, source_target_pairs={{1,0},{2,1},{3,2},{4,3},{5,4},{6,5},{7,6},{8,7},{9,8},{10,9},{11,1... | collective-permute-start | bytes 786440 | tf_op jit(solution)/shard_map/ppermute | solution.py:23
  121.1 11.0 %collective-permute-start.1 = (f32[1,256,256]{2,1,0:T(8,128)S(1)}, f32[1,256,256]{2,1,0:T(8,128)S(1)}, u32[]{:S(2)}, u32[]{:S(2)}) collective-permute-start(f32[1,256,256]{2,1,0:T(8,128)S(1)} %get-tuple-element.42), channel_id=1, source_target_pairs={{0,1},{1,2},{2,3},{3,4},{4,5},{5,6},{6,7},{7,8},{8,9},{9,10},{10,1... | collective-permute-start | bytes 786440 | tf_op jit(solution)/shard_map/ppermute | solution.py:21
  133.6 9.3 %collective-permute-start.2 = (f32[1,256,256]{2,1,0:T(8,128)S(1)}, f32[1,256,256]{2,1,0:T(8,128)S(1)}, u32[]{:S(2)}, u32[]{:S(2)}) collective-permute-start(f32[1,256,256]{2,1,0:T(8,128)S(1)} %get-tuple-element.31), channel_id=1, source_target_pairs={{1,0},{2,1},{3,2},{4,3},{5,4},{6,5},{7,6},{8,7},{9,8},{10,9},{11,1... | collective-permute-start | bytes 786440 | tf_op jit(solution)/shard_map/ppermute | solution.py:23
  138.3 10.5 %collective-permute-start.3 = (f32[1,256,256]{2,1,0:T(8,128)S(1)}, f32[1,256,256]{2,1,0:T(8,128)S(1)}, u32[]{:S(2)}, u32[]{:S(2)}) collective-permute-start(f32[1,256,256]{2,1,0:T(8,128)S(1)} %get-tuple-element.32), channel_id=1, source_target_pairs={{0,1},{1,2},{2,3},{3,4},{4,5},{5,6},{6,7},{7,8},{8,9},{9,10},{10,1... | collective-permute-start | bytes 786440 | tf_op jit(solution)/shard_map/ppermute | solution.py:21
  150.3 9.7 %collective-permute-start.4 = (f32[1,256,256]{2,1,0:T(8,128)S(1)}, f32[1,256,256]{2,1,0:T(8,128)S(1)}, u32[]{:S(2)}, u32[]{:S(2)}) collective-permute-start(f32[1,256,256]{2,1,0:T(8,128)S(1)} %get-tuple-element.21), channel_id=1, source_target_pairs={{1,0},{2,1},{3,2},{4,3},{5,4},{6,5},{7,6},{8,7},{9,8},{10,9},{11,1... | collective-permute-start | bytes 786440 | tf_op jit(solution)/shard_map/ppermute | solution.py:23
  155.7 10.9 %collective-permute-start.5 = (f32[1,256,256]{2,1,0:T(8,128)S(1)}, f32[1,256,256]{2,1,0:T(8,128)S(1)}, u32[]{:S(2)}, u32[]{:S(2)}) collective-permute-start(f32[1,256,256]{2,1,0:T(8,128)S(1)} %get-tuple-element.22), channel_id=1, source_target_pairs={{0,1},{1,2},{2,3},{3,4},{4,5},{5,6},{6,7},{7,8},{8,9},{9,10},{10,1... | collective-permute-start | bytes 786440 | tf_op jit(solution)/shard_map/ppermute | solution.py:21
  168.1 10.1 %collective-permute-start.6 = (f32[1,256,256]{2,1,0:T(8,128)S(1)}, f32[1,256,256]{2,1,0:T(8,128)S(1)}, u32[]{:S(2)}, u32[]{:S(2)}) collective-permute-start(f32[1,256,256]{2,1,0:T(8,128)S(1)} %get-tuple-element.19), channel_id=1, source_target_pairs={{1,0},{2,1},{3,2},{4,3},{5,4},{6,5},{7,6},{8,7},{9,8},{10,9},{11,1... | collective-permute-start | bytes 786440 | tf_op jit(solution)/shard_map/ppermute | solution.py:23
  173.6 10.8 %collective-permute-start.7 = (f32[1,256,256]{2,1,0:T(8,128)S(1)}, f32[1,256,256]{2,1,0:T(8,128)S(1)}, u32[]{:S(2)}, u32[]{:S(2)}) collective-permute-start(f32[1,256,256]{2,1,0:T(8,128)S(1)} %get-tuple-element.20), channel_id=1, source_target_pairs={{0,1},{1,2},{2,3},{3,4},{4,5},{5,6},{6,7},{7,8},{8,9},{9,10},{10,1... | collective-permute-start | bytes 786440 | tf_op jit(solution)/shard_map/ppermute | solution.py:21
Sparse Core Ops, SparseCore 0:
  9.2 98.3 all-gather.1
where the time goes:
time: 194 us; the launch traced here: 193 us
  waiting for transfers between devices  141 us (73%)
  starting transfers between devices  21.1 us (11%)
  between operations  14.2 us (7%)
  other arithmetic  12.9 us (7%)
  local copies, waits for them, and re-layouts  4.45 us (2%)
    all_gather x1, waiting for transfers between devices, local(): piece = lax.all_gather(field, 'rep', axis=0, tiled=True)  97.5 us
    ppermute x4, waiting for transfers between devices, padded_2(): lax.ppermute(tail, axis, [(i, (i + 1) % count) for i in range(count)])  24.2 us
    ppermute x4, starting transfers between devices, padded_2(): lax.ppermute(head, axis, [((i + 1) % count, i) for i in range(count)])  21.1 us
    ppermute x4, waiting for transfers between devices, padded_2(): lax.ppermute(head, axis, [((i + 1) % count, i) for i in range(count)])  18.2 us
    reduce_sum x1, other arithmetic, local(): start = jnp.sum(weight[:, None, None, None] * piece, axis=0, keepdims=True)  7.36 us
  transfers between devices with their start and end apart: 9, of which 9 were waited for; matrix products, arithmetic and copies ran while one was open for 2% of the time, Pallas kernels for 0%

commit v1 on v0

v1 whole, which is shorter than its diff:
```python
import jax
import jax.numpy as jnp
from jax import lax
from jax.experimental import pallas as pl
from jax.experimental.pallas import tpu as pltpu
from jax.sharding import PartitionSpec as P

STEPS = 4
KAPPA = 0.16
LAMBDA = 0.015
EPS = 0.75

MESH = pl.DeviceIdType.MESH
SLOTS = 4
ROWS = 32
PAD = 8
ALL = ROWS + 2 * PAD
LANES = 256
PAIRS = 4
CHUNKS = 16
LAG = 2
MESSAGES = CHUNKS + LAG
ORDER = (0, 2, 1, 3)


def kernel(field, momenta, counts, accept, out, own, send_up, send_down, from_below, from_above, phi0, phi1, phi2, phi3, mom,
           done, flag, flags, a_ss, a_rs, c_ss, c_rs, f_ss, f_rs, up_ss, up_rs, down_ss, down_rs, z_ss, z_rs, zm_ss, zm_rs,
           r_ss, r_rs, rz_ss, rz_rs, d_ss, d_rs, e_ss, e_rs, here):
    rep, gz = lax.axis_index("rep"), lax.axis_index("gz")
    y, z = rep // 4, gz // 2
    q = (gz % 2) * 4 + rep % 4
    slot, half = rep % 4, gz % 2

    def place(ring, row, depth):
        return (row * 4 + ring % 4, depth * 2 + ring // 4)

    def ring(step):
        return place((q + step + 8) % 8, y, z)

    above, below = place(q, (y + 1) % 4, z), place(q, (y + 3) % 4, z)
    z_next, z_last = place(q, y, (z + 1) % 8), place(q, y, (z + 7) % 8)

    def remote(src, dst, ss, rs, device):
        return pltpu.make_async_remote_copy(src_ref=src, dst_ref=dst, send_sem=ss, recv_sem=rs, device_id=device, device_id_type=MESH)

    barrier = pltpu.get_barrier_semaphore()
    partners = [ring(step) for step in range(1, 8)] + [above, below, z_next, z_last]
    for device in partners:
        pl.semaphore_signal(barrier, inc=1, device_id=device, device_id_type=MESH)
    pl.semaphore_wait(barrier, len(partners))

    def rows_of(place_):
        return pl.ds(pl.multiple_of(place_ * ROWS, ROWS), ROWS)

    def local_plane(pair):
        return pair + half * (3 - 2 * pair)

    def field_copy(pair, step):
        src = field.at[0, local_plane(pair), rows_of((q + step) % 8)]
        dst = own.at[pair, half, slot]
        if step == 0:
            return pltpu.make_async_copy(src, dst, a_rs.at[pair, 0])
        return remote(src, dst, a_ss.at[pair, step], a_rs.at[pair, step], ring(step))

    def momenta_copy(pair, step):
        src = momenta.at[0, local_plane(pair), rows_of((q + step) % 8)]
        dst = mom.at[slot, 4 + half * 4 + local_plane(pair)]
        if step == 0:
            return pltpu.make_async_copy(src, dst, c_rs.at[pair, 0])
        return remote(src, dst, c_ss.at[pair, step], c_rs.at[pair, step], ring(step))

    def flag_copy(step):
        if step == 0:
            return pltpu.make_async_copy(flag, flags.at[q], f_rs.at[0])
        return remote(flag, flags.at[q], f_ss.at[step], f_rs.at[step], ring(step))

    for pair in range(PAIRS):
        for step in range(8):
            field_copy(pair, step).start()
    flag[...] = jnp.full(flag.shape, accept[0], jnp.int32)
    for step in range(8):
        flag_copy(step).start()

    alive = [[(counts[4 * ((y + d) % 4) + i] > 0).astype(jnp.int32) for i in range(4)] for d in range(4)]
    before = [[sum(alive[d][:i], jnp.int32(0)) for i in range(4)] for d in range(4)]
    total = [sum(alive[d], jnp.int32(0)) for d in range(4)]
    mine = [jnp.int32(-1)] * 4
    for c in range(4):
        for i in range(4):
            mine[c] = jnp.where((alive[0][i] == 1) & (before[0][i] == c), i, mine[c])
    split_up = jnp.minimum(total[3], 4 - total[2])
    split = jnp.minimum(total[2], 4 - total[1])
    cum, parent = jnp.int32(0), [jnp.int32(0)] * SLOTS
    for r in range(16):
        cum = cum + counts[r]
        for s in range(SLOTS):
            parent[s] = parent[s] + (cum <= 4 * y + s).astype(jnp.int32)
    code = []
    for s in range(SLOTS):
        value = jnp.int32(0)
        for d in range(4):
            for i in range(4):
                k = before[d][i]
                if d == 0:
                    way = jnp.int32(i)
                elif d == 1:
                    way = 4 + k
                elif d == 3:
                    way = 8 + k
                else:
                    way = jnp.where(k < split, 12 + total[1] + k, 16 + total[3] + k - split)
                value = jnp.where(parent[s] == 4 * ((y + d) % 4) + i, way, value)
        code.append(value)

    def same(value, number):
        return jnp.full((8, LANES), value, jnp.int32) == number

    def octet(t):
        return t // 4, pl.ds(pl.multiple_of((t % 4) * 8, 8), 8)

    def assemble(t, forward):
        pair, rows = octet(jnp.minimum(t, CHUNKS - 1))
        for c in range(4):
            own_here = [same(mine[c], i) for i in range(4)]
            down_here = [same(total[0], c - f) for f in range(c + 1)]
            up_here = [same(split_up + c - total[0], f) for f in range(4)]
            for h in range(2):
                pieces = [own[pair, h, i, rows, :] for i in range(4)]
                if forward:
                    down, up = from_above[t - LAG, 0, h], from_below[t - LAG, 0, h]
                    for f in range(1, c + 1):
                        down = jnp.where(down_here[f], from_above[t - LAG, f, h], down)
                    for f in range(1, 4):
                        up = jnp.where(up_here[f], from_below[t - LAG, f, h], up)
                else:
                    down = up = pieces[0]
                for i in range(4):
                    down = jnp.where(own_here[i], pieces[i], down)
                    up = jnp.where(own_here[i], pieces[i], up)
                send_down[t, c, h] = down
                send_up[t, c, h] = up

    def up_copy(t):
        return remote(send_up.at[t], from_below.at[t], up_ss.at[t], up_rs.at[t], above)

    def down_copy(t):
        return remote(send_down.at[t], from_above.at[t], down_ss.at[t], down_rs.at[t], below)

    def pick(u):
        pair, rows = octet(u)
        target = pl.ds(pl.multiple_of(PAD + (u % 4) * 8, 8), 8)
        for s in range(SLOTS):
            here_ = [same(code[s], k) for k in range(20)]
            for h in range(2):
                value = own[pair, h, 0, rows, :]
                for i in range(1, 4):
                    value = jnp.where(here_[i], own[pair, h, i, rows, :], value)
                for c in range(4):
                    value = jnp.where(here_[4 + c], from_above[u, c, h], value)
                    value = jnp.where(here_[8 + c], from_below[u, c, h], value)
                    value = jnp.where(here_[12 + c], from_above[u + LAG, c, h], value)
                    value = jnp.where(here_[16 + c], from_below[u + LAG, c, h], value)
                plane = 4 + pair if h == 0 else 11 - pair
                phi0[s, plane, target, :] = value

    inner = pl.ds(PAD, ROWS)
    first, last = pl.ds(PAD, PAD), pl.ds(ROWS, PAD)
    low, high = pl.ds(0, PAD), pl.ds(PAD + ROWS, PAD)

    def z_copies(pair):
        return (
            remote(phi0.at[:, 4 + pair, inner], phi0.at[:, 12 + pair, inner], z_ss.at[pair, 0], z_rs.at[pair, 0], z_last),
            remote(phi0.at[:, 11 - pair, inner], phi0.at[:, 3 - pair, inner], z_ss.at[pair, 1], z_rs.at[pair, 1], z_next),
        )

    def zm_copies(pair):
        return (
            remote(mom.at[:, 4 + pair], mom.at[:, 12 + pair], zm_ss.at[pair, 0], zm_rs.at[pair, 0], z_last),
            remote(mom.at[:, 11 - pair], mom.at[:, 3 - pair], zm_ss.at[pair, 1], zm_rs.at[pair, 1], z_next),
        )

    def row_copies(planes, ss, rs):
        copies = []
        for n, plane in enumerate(planes):
            copies.append(remote(phi0.at[:, plane, first], phi0.at[:, plane, high], ss.at[n, 0], rs.at[n, 0], ring(-1)))
            copies.append(remote(phi0.at[:, plane, last], phi0.at[:, plane, low], ss.at[n, 1], rs.at[n, 1], ring(1)))
        return copies

    def own_rows(pair):
        return row_copies((4 + pair, 11 - pair), r_ss.at[pair], r_rs.at[pair])

    def halo_rows(pair):
        return row_copies((12 + pair, 3 - pair), rz_ss.at[pair], rz_rs.at[pair])

    def tick(t, carry):
        @pl.when((t % 4 == 0) & (t < CHUNKS))
        def _():
            for step in range(8):
                copy = field_copy(t // 4, step)
                copy.wait() if step == 0 else copy.wait_recv()

        @pl.when(t >= LAG)
        def _():
            up_copy(t - LAG).wait_recv()
            down_copy(t - LAG).wait_recv()

        @pl.when(t < LAG)
        def _():
            assemble(t, False)

        @pl.when((t >= LAG) & (t < MESSAGES))
        def _():
            assemble(t, True)

        @pl.when(t < MESSAGES)
        def _():
            up_copy(t).start()
            down_copy(t).start()

        @pl.when((t >= 6) & (t < 14) & (t % 2 == 0))
        def _():
            for step in range(8):
                momenta_copy((t - 6) // 2, step).start()

        @pl.when(t >= 2 * LAG)
        def _():
            pick(t - 2 * LAG)

        @pl.when((t >= 7) & (t % 4 == 3))
        def _():
            for copy in z_copies((t - 7) // 4) + tuple(own_rows((t - 7) // 4)):
                copy.start()

        @pl.when((t == 11) | (t == 13) | (t == 15))
        def _():
            pair = (t - 11) // 2
            for step in range(8):
                copy = momenta_copy(pair, step)
                copy.wait() if step == 0 else copy.wait_recv()
            for copy in zm_copies(pair):
                copy.start()

        @pl.when((t == 10) | (t == 14) | (t == 18))
        def _():
            pair = (t - 10) // 4
            for copy in z_copies(pair):
                copy.wait_recv()
            for copy in halo_rows(pair):
                copy.start()

        return carry

    lax.fori_loop(0, MESSAGES + LAG, tick, 0)

    for step in range(8):
        copy = momenta_copy(3, step)
        copy.wait() if step == 0 else copy.wait_recv()
        copy = flag_copy(step)
        copy.wait() if step == 0 else copy.wait_recv()
    for pair in range(3):
        for copy in zm_copies(pair):
            copy.wait()
        for copy in tuple(own_rows(pair)) + tuple(halo_rows(pair)):
            copy.wait_recv()
    for copy in z_copies(3) + tuple(own_rows(3)):
        copy.wait_recv()

    phis = (phi0, phi1, phi2, phi3)

    def edge_copies(k, s):
        planes = pl.ds(k + 1, 14 - 2 * k)
        ref = phis[k]
        return (
            remote(ref.at[s, planes, first], ref.at[s, planes, high], d_ss.at[k, s, 0], d_rs.at[k, s, 0], ring(-1)),
            remote(ref.at[s, planes, last], ref.at[s, planes, low], d_ss.at[k, s, 1], d_rs.at[k, s, 1], ring(1)),
        )

    def result_copy(s, h):
        return remote(done.at[s, pl.ds(4 * h, 4)], out.at[0, :, rows_of(q)], e_ss.at[s, h], e_rs.at[q], place(4 * h + s, y, z))

    def result_here(s, h):
        return pltpu.make_async_copy(done.at[s, pl.ds(4 * h, 4)], out.at[0, :, rows_of(q)], here)

    for k in range(1, STEPS + 1):
        for s in ORDER:
            if k > 1:
                for copy in edge_copies(k - 1, s):
                    copy.wait_recv()
            phi = phis[k - 1]
            if k == STEPS:
                tile = flags[s] == 1
                taken = jnp.concatenate([tile] * (ROWS // 8), axis=0)

            def plane_step(plane, carry):
                centre = phi[s, plane, inner, :]
                beside = phi[s, plane - 1, inner, :] + phi[s, plane + 1, inner, :]
                beside = beside + phi[s, plane, pl.ds(PAD - 1, ROWS), :] + phi[s, plane, pl.ds(PAD + 1, ROWS), :]
                beside = beside + pltpu.roll(centre, 1, 1) + pltpu.roll(centre, LANES - 1, 1)
                force = 2.0 * KAPPA * beside - 2.0 * centre - 4.0 * LAMBDA * centre * (centre * centre - 1.0)
                moved = mom[s, plane] + (0.5 * EPS if k == 1 else EPS) * force
                value = centre + EPS * moved
                if k < STEPS:
                    mom[s, plane] = moved
                    phis[k][s, plane, inner, :] = value
                else:
                    done[s, plane - 4] = jnp.where(taken, value, phi0[s, plane, inner, :])
                return carry

            lax.fori_loop(k, 16 - k, plane_step, 0)
            if k < STEPS:
                for copy in edge_copies(k, s):
                    copy.start()
            else:
                for h in range(2):
                    @pl.when(q == 4 * h + s)
                    def _():
                        result_here(s, h).start()

                    @pl.when(q != 4 * h + s)
                    def _():
                        result_copy(s, h).start()

    for pair in range(PAIRS):
        for step in range(1, 8):
            field_copy(pair, step).wait_send()
            momenta_copy(pair, step).wait_send()
        for copy in z_copies(pair) + tuple(own_rows(pair)):
            copy.wait_send()
    for step in range(1, 8):
        flag_copy(step).wait_send()
    for pair in range(3):
        for copy in halo_rows(pair):
            copy.wait_send()

    def left(t, carry):
        up_copy(t).wait_send()
        down_copy(t).wait_send()
        return carry

    lax.fori_loop(0, MESSAGES, left, 0)
    for k in range(1, STEPS):
        for s in range(SLOTS):
            for copy in edge_copies(k, s):
                copy.wait_send()
    for s in range(SLOTS):
        for h in range(2):
            @pl.when(q == 4 * h + s)
            def _():
                result_here(s, h).wait()

            @pl.when(q != 4 * h + s)
            def _():
                result_copy(s, h).wait_send()
    for step in range(1, 8):
        origin = (q + 8 - step) % 8
        remote(done.at[0, pl.ds(0, 4)], out.at[0, :, rows_of(origin)], e_ss.at[0, 0], e_rs.at[origin], ring(step)).wait_recv()


def local(field, momenta, counts, accept):
    f32, dma = jnp.float32, pltpu.SemaphoreType.DMA
    message = (MESSAGES, 4, 2, 8, LANES)
    return pl.pallas_call(
        kernel,
        out_shape=jax.ShapeDtypeStruct(field.shape, f32),
        in_specs=[
            pl.BlockSpec(memory_space=pl.ANY),
            pl.BlockSpec(memory_space=pl.ANY),
            pl.BlockSpec(memory_space=pltpu.SMEM),
            pl.BlockSpec(memory_space=pltpu.SMEM),
        ],
        out_specs=pl.BlockSpec(memory_space=pltpu.VMEM),
        scratch_shapes=[
            pltpu.VMEM((PAIRS, 2, SLOTS, ROWS, LANES), f32),
            pltpu.VMEM(message, f32),
            pltpu.VMEM(message, f32),
            pltpu.VMEM(message, f32),
            pltpu.VMEM(message, f32),
            pltpu.VMEM((SLOTS, 16, ALL, LANES), f32),
            pltpu.VMEM((SLOTS, 16, ALL, LANES), f32),
            pltpu.VMEM((SLOTS, 16, ALL, LANES), f32),
            pltpu.VMEM((SLOTS, 16, ALL, LANES), f32),
            pltpu.VMEM((SLOTS, 16, ROWS, LANES), f32),
            pltpu.VMEM((SLOTS, 8, ROWS, LANES), f32),
            pltpu.VMEM((8, LANES), jnp.int32),
            pltpu.VMEM((8, 8, LANES), jnp.int32),
            dma((PAIRS, 8)), dma((PAIRS, 8)), dma((PAIRS, 8)), dma((PAIRS, 8)), dma((8,)), dma((8,)),
            dma((MESSAGES,)), dma((MESSAGES,)), dma((MESSAGES,)), dma((MESSAGES,)),
            dma((PAIRS, 2)), dma((PAIRS, 2)), dma((3, 2)), dma((3, 2)),
            dma((PAIRS, 2, 2)), dma((PAIRS, 2, 2)), dma((3, 2, 2)), dma((3, 2, 2)),
            dma((STEPS, SLOTS, 2)), dma((STEPS, SLOTS, 2)), dma((SLOTS, 2)), dma((8,)), dma,
        ],
        compiler_params=pltpu.CompilerParams(collective_id=0, has_side_effects=True, vmem_limit_bytes=48 * 1024 * 1024),
    )(field, momenta, counts, accept)


def solution(mesh):
    placed = (P("rep", "gz", None, None), P("rep", "gz", None, None), P(), P("rep"))
    return jax.shard_map(
        local, mesh=mesh, in_specs=placed, out_specs=P("rep", "gz", None, None), check_vma=False
    )
```

time: 194 us -> 95.6 us (0.49)
  waiting for transfers between devices: 141 us -> 0 us
  Pallas kernels: 0 us -> 91.3 us
  starting transfers between devices: 21.1 us -> 0 us
  between operations: 14.2 us -> 0.69 us
  other arithmetic: 12.9 us -> 0 us
    all_gather x1 -> x0, waiting for transfers between devices: 97.5 us -> none  [local(): piece = lax.all_gather(field, 'rep', axis=0, tiled=True)]
    pallas_call x0 -> x1, Pallas kernels: none -> 91.3 us  [local(): pl.pallas_call(kernel, out_shape=jax.ShapeDtypeStruct(field.shape, f32),...]
    ppermute x8 -> x0, waiting for transfers between devices: 42.4 us -> none  [the longest x4 24.2 us: padded_2(): lax.ppermute(tail, axis, [(i, (i + 1) % count) for i in range(count)])]
    ppermute x8 -> x0, starting transfers between devices: 21.1 us -> none  [the longest x4 21.1 us: padded_2(): lax.ppermute(head, axis, [((i + 1) % count, i) for i in range(count)])]
    reduce_sum x2 -> x0, other arithmetic: 7.47 us -> none  [the longest x1 7.36 us: local(): start = jnp.sum(weight[:, None, None, None] * piece, axis=0, keepdims=True)]
    unnamed x2 -> x7, local copies, waits for them, and re-layouts: 0.01 us -> 3.42 us
    slice x20 -> x0, local copies, waits for them, and re-layouts: 3.12 us -> none  [the longest x8 2.23 us: force(): beside_all = beside_all + jnp.roll(phi, 1, 2) + jnp.roll(phi, -1, 2)]
    add x3 -> x0, other arithmetic: 2.7 us -> none  [local(): phi = phi + EPS * mom]
  transfers between devices with their start and end apart: 9 -> 0, of which waited for: 9 -> 0; matrix products, arithmetic and copies ran while one was open for 2% -> 0% of each run, Pallas kernels for 0% -> 0%
where the time goes in v1:
time: 95.6 us; the launch traced here: 95.4 us
  Pallas kernels  91.3 us (96%)
  local copies, waits for them, and re-layouts  3.42 us (4%)
    pallas_call x1, Pallas kernels, local(): pl.pallas_call(kernel, out_shape=jax.ShapeDtypeStruct(field.shape, f32),...  91.3 us
    unnamed x7, local copies, waits for them, and re-layouts  3.42 us

profile of v1, /device:TPU:1, one launch (start us, length us, event | category | flops | bytes accessed | tf_op | source)
XLA Modules:
  0.0 95.4 jit_solution(1726438173853716591)
XLA Ops:
  0.0 0.0 copy-start.2
  0.7 0.0 copy-done.2
  0.7 0.0 copy-start
  0.7 1.2 %copy-done = f32[1,4,256,256]{3,2,1,0:T(8,128)S(1)} copy-done((f32[1,4,256,256]{3,2,1,0:T(8,128)S(1)}, f32[1,4,256,256]{3,2,1,0:T(8,128)}, u32[]{:S(2)}) %copy-start) | copy-done | bytes 1048600
  1.9 0.0 copy-start.1
  1.9 1.2 %copy-done.1 = f32[1,4,256,256]{3,2,1,0:T(8,128)S(1)} copy-done((f32[1,4,256,256]{3,2,1,0:T(8,128)S(1)}, f32[1,4,256,256]{3,2,1,0:T(8,128)}, u32[]{:S(2)}) %copy-start.1) | copy-done | bytes 1048600
  3.1 91.3 %shard_map.46 = f32[1,4,256,256]{3,2,1,0:T(8,128)S(1)} custom-call(f32[1,4,256,256]{3,2,1,0:T(8,128)S(1)} %copy-done, f32[1,4,256,256]{3,2,1,0:T(8,128)S(1)} %copy-done.1, s32[16]{0:T(128)S(1)} %copy-done.2, s32[1]{0:T(128)S(6)} %copy.6.accept), custom_call_target="tpu_custom_call" | custom-call | tf_op jit(solution)/shard_map/pallas_call | solution.py:362
  94.5 1.0 %copy.7 = f32[1,4,256,256]{3,2,1,0:T(8,128)} copy(f32[1,4,256,256]{3,2,1,0:T(8,128)S(1)} %shard_map.46) | data formatting | bytes 2097152
Async XLA Ops:
  0.0 0.7 copy-start.2
  0.7 1.2 %copy-start = (f32[1,4,256,256]{3,2,1,0:T(8,128)S(1)}, f32[1,4,256,256]{3,2,1,0:T(8,128)}, u32[]{:S(2)}) copy-start(f32[1,4,256,256]{3,2,1,0:T(8,128)} %field.1) | copy-start | bytes 3145732
  1.9 1.2 %copy-start.1 = (f32[1,4,256,256]{3,2,1,0:T(8,128)S(1)}, f32[1,4,256,256]{3,2,1,0:T(8,128)}, u32[]{:S(2)}) copy-start(f32[1,4,256,256]{3,2,1,0:T(8,128)} %momenta.1) | copy-start | bytes 3145732

commit v2 on v1

--- a/solution.py
+++ b/solution.py
@@ -13,23 +13,28 @@
 MESH = pl.DeviceIdType.MESH
 SLOTS = 4
 ROWS = 32
-PAD = 8
+PAD = 4
 ALL = ROWS + 2 * PAD
 LANES = 256
 PAIRS = 4
 CHUNKS = 16
-LAG = 2
+LAG = 3
 MESSAGES = CHUNKS + LAG
 ORDER = (0, 2, 1, 3)
 
 
-def kernel(field, momenta, counts, accept, out, own, send_up, send_down, from_below, from_above, phi0, phi1, phi2, phi3, mom,
-           done, flag, flags, a_ss, a_rs, c_ss, c_rs, f_ss, f_rs, up_ss, up_rs, down_ss, down_rs, z_ss, z_rs, zm_ss, zm_rs,
-           r_ss, r_rs, rz_ss, rz_rs, d_ss, d_rs, e_ss, e_rs, here):
+def kernel(field, momenta, counts, accept, out, own, send_up, send_down, from_below, from_above, phi0, phi1, phi2, mom,
+           done, slab, edges, flag, flags, a_ss, a_rs, c_ss, c_rs, ch_ss, ch_rs, f_ss, f_rs, up_ss, up_rs, down_ss, down_rs, z_ss, z_rs, zm_ss, zm_rs,
+           r_ss, r_rs, e_ss, e_rs, here):
     rep, gz = lax.axis_index("rep"), lax.axis_index("gz")
     y, z = rep // 4, gz // 2
     q = (gz % 2) * 4 + rep % 4
     slot, half = rep % 4, gz % 2
+
+    inner = pl.ds(0, ROWS)
+    first, last = pl.ds(0, PAD), pl.ds(ROWS - PAD, PAD)
+    high, low = pl.ds(ROWS, PAD), pl.ds(ROWS + PAD, PAD)
+    beside_inner = pl.ds(ROWS, 2 * PAD)
 
     def place(ring, row, depth):
         return (row * 4 + ring % 4, depth * 2 + ring // 4)
@@ -64,19 +69,36 @@
 
     def momenta_copy(pair, step):
         src = momenta.at[0, local_plane(pair), rows_of((q + step) % 8)]
-        dst = mom.at[slot, 4 + half * 4 + local_plane(pair)]
+        dst = mom.at[slot, 4 + half * 4 + local_plane(pair), inner]
         if step == 0:
             return pltpu.make_async_copy(src, dst, c_rs.at[pair, 0])
         return remote(src, dst, c_ss.at[pair, step], c_rs.at[pair, step], ring(step))
+
+    def edge_copy(step):
+        src, dst = edges.at[step], mom.at[slot, pl.ds(4 + half * 4, 4), beside_inner]
+        if step == 0:
+            return pltpu.make_async_copy(src, dst, ch_rs.at[0])
+        return remote(src, dst, ch_ss.at[step], ch_rs.at[step], ring(step))
+
+    whole_momenta = pltpu.make_async_copy(momenta.at[0], slab, here)
+    whole_momenta.start()
+
+    def fill_edges():
+        upper = lax.broadcasted_iota(jnp.int32, (8, LANES), 0) < PAD
+        for step in range(8):
+            base = ((q + step) % 8) * ROWS
+            after = pl.ds(pl.multiple_of((base + ROWS) % 256, 8), 8)
+            ahead = pl.ds(pl.multiple_of((base + 248) % 256, 8), 8)
+            for plane in range(4):
+                edges[step, plane] = jnp.where(upper, slab[plane, after, :], slab[plane, ahead, :])
 
     def flag_copy(step):
         if step == 0:
             return pltpu.make_async_copy(flag, flags.at[q], f_rs.at[0])
         return remote(flag, flags.at[q], f_ss.at[step], f_rs.at[step], ring(step))
 
-    for pair in range(PAIRS):
-        for step in range(8):
-            field_copy(pair, step).start()
+    for step in range(8):
+        field_copy(0, step).start()
     flag[...] = jnp.full(flag.shape, accept[0], jnp.int32)
     for step in range(8):
         flag_copy(step).start()
@@ -148,7 +170,6 @@
 
     def pick(u):
         pair, rows = octet(u)
-        target = pl.ds(pl.multiple_of(PAD + (u % 4) * 8, 8), 8)
         for s in range(SLOTS):
             here_ = [same(code[s], k) for k in range(20)]
             for h in range(2):
@@ -161,16 +182,12 @@
                     value = jnp.where(here_[12 + c], from_above[u + LAG, c, h], value)
                     value = jnp.where(here_[16 + c], from_below[u + LAG, c, h], value)
                 plane = 4 + pair if h == 0 else 11 - pair
-                phi0[s, plane, target, :] = value
-
-    inner = pl.ds(PAD, ROWS)
-    first, last = pl.ds(PAD, PAD), pl.ds(ROWS, PAD)
-    low, high = pl.ds(0, PAD), pl.ds(PAD + ROWS, PAD)
-
-    def z_copies(pair):
+                phi0[s, plane, rows, :] = value
+
+    def z_copies(pair, rows):
         return (
-            remote(phi0.at[:, 4 + pair, inner], phi0.at[:, 12 + pair, inner], z_ss.at[pair, 0], z_rs.at[pair, 0], z_last),
-            remote(phi0.at[:, 11 - pair, inner], phi0.at[:, 3 - pair, inner], z_ss.at[pair, 1], z_rs.at[pair, 1], z_next),
+            remote(phi0.at[:, 4 + pair, rows], phi0.at[:, 12 + pair, rows], z_ss.at[pair, 0], z_rs.at[pair, 0], z_last),
+            remote(phi0.at[:, 11 - pair, rows], phi0.at[:, 3 - pair, rows], z_ss.at[pair, 1], z_rs.at[pair, 1], z_next),
         )
 
     def zm_copies(pair):
@@ -179,20 +196,23 @@
             remote(mom.at[:, 11 - pair], mom.at[:, 3 - pair], zm_ss.at[pair, 1], zm_rs.at[pair, 1], z_next),
         )
 
-    def row_copies(planes, ss, rs):
+    def row_copies(pair):
         copies = []
-        for n, plane in enumerate(planes):
-            copies.append(remote(phi0.at[:, plane, first], phi0.at[:, plane, high], ss.at[n, 0], rs.at[n, 0], ring(-1)))
-            copies.append(remote(phi0.at[:, plane, last], phi0.at[:, plane, low], ss.at[n, 1], rs.at[n, 1], ring(1)))
+        for n, plane in enumerate((4 + pair, 11 - pair)):
+            copies.append(remote(phi0.at[:, plane, first], phi0.at[:, plane, high], r_ss.at[pair, n, 0], r_rs.at[pair, n, 0], ring(-1)))
+            copies.append(remote(phi0.at[:, plane, last], phi0.at[:, plane, low], r_ss.at[pair, n, 1], r_rs.at[pair, n, 1], ring(1)))
         return copies
 
-    def own_rows(pair):
-        return row_copies((4 + pair, 11 - pair), r_ss.at[pair], r_rs.at[pair])
-
-    def halo_rows(pair):
-        return row_copies((12 + pair, 3 - pair), rz_ss.at[pair], rz_rs.at[pair])
+    whole = pl.ds(0, ALL)
 
     def tick(t, carry):
+        @pl.when((t < 6) & (t % 2 == 0))
+        def _():
+            for step in range(1, 8):
+                field_copy(t // 2, step).wait_send()
+            for step in range(8):
+                field_copy(t // 2 + 1, step).start()
+
         @pl.when((t % 4 == 0) & (t < CHUNKS))
         def _():
             for step in range(8):
@@ -217,6 +237,13 @@
             up_copy(t).start()
             down_copy(t).start()
 
+        @pl.when(t == 6)
+        def _():
+            whole_momenta.wait()
+            fill_edges()
+            for step in range(8):
+                edge_copy(step).start()
+
         @pl.when((t >= 6) & (t < 14) & (t % 2 == 0))
         def _():
             for step in range(8):
@@ -226,32 +253,40 @@
         def _():
             pick(t - 2 * LAG)
 
-        @pl.when((t >= 7) & (t % 4 == 3))
-        def _():
-            for copy in z_copies((t - 7) // 4) + tuple(own_rows((t - 7) // 4)):
+        @pl.when((t >= 2 * LAG + 3) & ((t - 2 * LAG) % 4 == 3))
+        def _():
+            for copy in row_copies((t - 2 * LAG - 3) // 4):
                 copy.start()
 
-        @pl.when((t == 11) | (t == 13) | (t == 15))
-        def _():
-            pair = (t - 11) // 2
+        @pl.when((t >= 2 * LAG + 5) & ((t - 2 * LAG) % 4 == 1))
+        def _():
+            pair = (t - 2 * LAG - 5) // 4
+            for copy in row_copies(pair):
+                copy.wait_recv()
+            for copy in z_copies(pair, whole):
+                copy.start()
+
+        @pl.when(t == 12)
+        def _():
+            for step in range(8):
+                copy = edge_copy(step)
+                copy.wait() if step == 0 else copy.wait_recv()
+
+        @pl.when((t == 12) | (t == 14) | (t == 16))
+        def _():
+            pair = (t - 12) // 2
             for step in range(8):
                 copy = momenta_copy(pair, step)
                 copy.wait() if step == 0 else copy.wait_recv()
             for copy in zm_copies(pair):
                 copy.start()
 
-        @pl.when((t == 10) | (t == 14) | (t == 18))
-        def _():
-            pair = (t - 10) // 4
-            for copy in z_copies(pair):
-                copy.wait_recv()
-            for copy in halo_rows(pair):
-                copy.start()
-
         return carry
 
     lax.fori_loop(0, MESSAGES + LAG, tick, 0)
 
+    for copy in z_copies(3, inner):
+        copy.start()
     for step in range(8):
         copy = momenta_copy(3, step)
         copy.wait() if step == 0 else copy.wait_recv()
@@ -260,20 +295,10 @@
     for pair in range(3):
         for copy in zm_copies(pair):
             copy.wait()
-        for copy in tuple(own_rows(pair)) + tuple(halo_rows(pair)):
+        for copy in z_copies(pair, whole):
             copy.wait_recv()
-    for copy in z_copies(3) + tuple(own_rows(3)):
+    for copy in z_copies(3, inner) + tuple(row_copies(3)):
         copy.wait_recv()
-
-    phis = (phi0, phi1, phi2, phi3)
-
-    def edge_copies(k, s):
-        planes = pl.ds(k + 1, 14 - 2 * k)
-        ref = phis[k]
-        return (
-            remote(ref.at[s, planes, first], ref.at[s, planes, high], d_ss.at[k, s, 0], d_rs.at[k, s, 0], ring(-1)),
-            remote(ref.at[s, planes, last], ref.at[s, planes, low], d_ss.at[k, s, 1], d_rs.at[k, s, 1], ring(1)),
-        )
 
     def result_copy(s, h):
         return remote(done.at[s, pl.ds(4 * h, 4)], out.at[0, :, rows_of(q)], e_ss.at[s, h], e_rs.at[q], place(4 * h + s, y, z))
@@ -281,56 +306,47 @@
     def result_here(s, h):
         return pltpu.make_async_copy(done.at[s, pl.ds(4 * h, 4)], out.at[0, :, rows_of(q)], here)
 
-    for k in range(1, STEPS + 1):
-        for s in ORDER:
-            if k > 1:
-                for copy in edge_copies(k - 1, s):
-                    copy.wait_recv()
-            phi = phis[k - 1]
-            if k == STEPS:
-                tile = flags[s] == 1
-                taken = jnp.concatenate([tile] * (ROWS // 8), axis=0)
+    def force(centre, beside):
+        beside = beside + pltpu.roll(centre, 1, 0) + pltpu.roll(centre, ALL - 1, 0)
+        beside = beside + pltpu.roll(centre, 1, 1) + pltpu.roll(centre, LANES - 1, 1)
+        return 2.0 * KAPPA * beside - 2.0 * centre - 4.0 * LAMBDA * centre * (centre * centre - 1.0)
+
+    for s in ORDER:
+        steps = (phi0.at[s], phi1, phi2, phi1)
+        taken = jnp.concatenate([flags[s] == 1] * (ROWS // 8), axis=0)
+        for k in range(1, STEPS + 1):
+            phi = steps[k - 1]
 
             def plane_step(plane, carry):
-                centre = phi[s, plane, inner, :]
-                beside = phi[s, plane - 1, inner, :] + phi[s, plane + 1, inner, :]
-                beside = beside + phi[s, plane, pl.ds(PAD - 1, ROWS), :] + phi[s, plane, pl.ds(PAD + 1, ROWS), :]
-                beside = beside + pltpu.roll(centre, 1, 1) + pltpu.roll(centre, LANES - 1, 1)
-                force = 2.0 * KAPPA * beside - 2.0 * centre - 4.0 * LAMBDA * centre * (centre * centre - 1.0)
-                moved = mom[s, plane] + (0.5 * EPS if k == 1 else EPS) * force
+                centre = phi[plane]
+                moved = mom[s, plane] + (0.5 * EPS if k == 1 else EPS) * force(centre, phi[plane - 1] + phi[plane + 1])
                 value = centre + EPS * moved
                 if k < STEPS:
                     mom[s, plane] = moved
-                    phis[k][s, plane, inner, :] = value
+                    steps[k][plane] = value
                 else:
-                    done[s, plane - 4] = jnp.where(taken, value, phi0[s, plane, inner, :])
+                    done[s, plane - 4] = jnp.where(taken, value[:ROWS], phi0[s, plane, inner, :])
                 return carry
 
-            lax.fori_loop(k, 16 - k, plane_step, 0)
-            if k < STEPS:
-                for copy in edge_copies(k, s):
-                    copy.start()
-            else:
-                for h in range(2):
-                    @pl.when(q == 4 * h + s)
-                    def _():
-                        result_here(s, h).start()
-
-                    @pl.when(q != 4 * h + s)
-                    def _():
-                        result_copy(s, h).start()
+            lax.fori_loop(k, 16 - k, plane_step, 0, unroll=2)
+        for h in range(2):
+            @pl.when(q == 4 * h + s)
+            def _():
+                result_here(s, h).start()
+
+            @pl.when(q != 4 * h + s)
+            def _():
+                result_copy(s, h).start()
 
     for pair in range(PAIRS):
         for step in range(1, 8):
-            field_copy(pair, step).wait_send()
             momenta_copy(pair, step).wait_send()
-        for copy in z_copies(pair) + tuple(own_rows(pair)):
+        for copy in z_copies(pair, whole if pair < 3 else inner) + tuple(row_copies(pair)):
             copy.wait_send()
     for step in range(1, 8):
         flag_copy(step).wait_send()
-    for pair in range(3):
-        for copy in halo_rows(pair):
-            copy.wait_send()
+        field_copy(3, step).wait_send()
+        edge_copy(step).wait_send()
 
     def left(t, carry):
         up_copy(t).wait_send()
@@ -338,10 +354,6 @@
         return carry
 
     lax.fori_loop(0, MESSAGES, left, 0)
-    for k in range(1, STEPS):
-        for s in range(SLOTS):
-            for copy in edge_copies(k, s):
-                copy.wait_send()
     for s in range(SLOTS):
         for h in range(2):
             @pl.when(q == 4 * h + s)
@@ -363,12 +375,12 @@
         kernel,
         out_shape=jax.ShapeDtypeStruct(field.shape, f32),
         in_specs=[
-            pl.BlockSpec(memory_space=pl.ANY),
-            pl.BlockSpec(memory_space=pl.ANY),
+            pl.BlockSpec(memory_space=pltpu.HBM),
+            pl.BlockSpec(memory_space=pltpu.HBM),
             pl.BlockSpec(memory_space=pltpu.SMEM),
             pl.BlockSpec(memory_space=pltpu.SMEM),
         ],
-        out_specs=pl.BlockSpec(memory_space=pltpu.VMEM),
+        out_specs=pl.BlockSpec(memory_space=pl.ANY),
         scratch_shapes=[
             pltpu.VMEM((PAIRS, 2, SLOTS, ROWS, LANES), f32),
             pltpu.VMEM(message, f32),
@@ -376,20 +388,20 @@
             pltpu.VMEM(message, f32),
             pltpu.VMEM(message, f32),
             pltpu.VMEM((SLOTS, 16, ALL, LANES), f32),
+            pltpu.VMEM((16, ALL, LANES), f32),
+            pltpu.VMEM((16, ALL, LANES), f32),
             pltpu.VMEM((SLOTS, 16, ALL, LANES), f32),
-            pltpu.VMEM((SLOTS, 16, ALL, LANES), f32),
-            pltpu.VMEM((SLOTS, 16, ALL, LANES), f32),
-            pltpu.VMEM((SLOTS, 16, ROWS, LANES), f32),
             pltpu.VMEM((SLOTS, 8, ROWS, LANES), f32),
+            pltpu.VMEM((4, 256, LANES), f32),
+            pltpu.VMEM((8, 4, 8, LANES), f32),
             pltpu.VMEM((8, LANES), jnp.int32),
             pltpu.VMEM((8, 8, LANES), jnp.int32),
-            dma((PAIRS, 8)), dma((PAIRS, 8)), dma((PAIRS, 8)), dma((PAIRS, 8)), dma((8,)), dma((8,)),
+            dma((PAIRS, 8)), dma((PAIRS, 8)), dma((PAIRS, 8)), dma((PAIRS, 8)), dma((8,)), dma((8,)), dma((8,)), dma((8,)),
             dma((MESSAGES,)), dma((MESSAGES,)), dma((MESSAGES,)), dma((MESSAGES,)),
             dma((PAIRS, 2)), dma((PAIRS, 2)), dma((3, 2)), dma((3, 2)),
-            dma((PAIRS, 2, 2)), dma((PAIRS, 2, 2)), dma((3, 2, 2)), dma((3, 2, 2)),
-            dma((STEPS, SLOTS, 2)), dma((STEPS, SLOTS, 2)), dma((SLOTS, 2)), dma((8,)), dma,
+            dma((PAIRS, 2, 2)), dma((PAIRS, 2, 2)), dma((SLOTS, 2)), dma((8,)), dma,
         ],
-        compiler_params=pltpu.CompilerParams(collective_id=0, has_side_effects=True, vmem_limit_bytes=48 * 1024 * 1024),
+        compiler_params=pltpu.CompilerParams(collective_id=0, has_side_effects=True, vmem_limit_bytes=60 * 1024 * 1024),
     )(field, momenta, counts, accept)
 
 

time: 95.6 us -> 82.9 us (0.87)
  Pallas kernels: 91.3 us -> 79.2 us
  local copies, waits for them, and re-layouts: 3.42 us -> 2.29 us
    pallas_call x1, Pallas kernels: 91.3 us -> 79.2 us  [local(): pl.pallas_call(kernel, out_shape=jax.ShapeDtypeStruct(field.shape, f32),...]
    unnamed x7 -> x1, local copies, waits for them, and re-layouts: 3.42 us -> 2.29 us
where the time goes in v2:
time: 82.9 us; the launch traced here: 82.1 us
  Pallas kernels  79.2 us (96%)
  local copies, waits for them, and re-layouts  2.29 us (3%)
    pallas_call x1, Pallas kernels, local(): pl.pallas_call(kernel, out_shape=jax.ShapeDtypeStruct(field.shape, f32),...  79.2 us
    unnamed x1, local copies, waits for them, and re-layouts  2.29 us

profile of v2, /device:TPU:1, one launch (start us, length us, event | category | flops | bytes accessed | tf_op | source)
XLA Modules:
  0.0 82.1 jit_solution(6092876314012152096)
XLA Ops:
  0.7 79.2 %shard_map.46 = f32[1,4,256,256]{3,2,1,0:T(8,128)} custom-call(f32[1,4,256,256]{3,2,1,0:T(8,128)} %field.1, f32[1,4,256,256]{3,2,1,0:T(8,128)} %momenta.1, s32[16]{0:T(128)} %counts.1, s32[1]{0:T(128)S(6)} %copy.6.accept), custom_call_target="tpu_custom_call" | custom-call | tf_op jit(solution)/shard_map/pallas_call | solution.py:374
  79.8 2.3 %copy.7 = f32[1,4,256,256]{3,2,1,0:T(8,128)} copy(f32[1,4,256,256]{3,2,1,0:T(8,128)} %shard_map.46) | data formatting | bytes 2097152

commit v3 on v2

v3 whole, which is shorter than its diff:
```python
import jax
import jax.numpy as jnp
from jax import lax
from jax.experimental import pallas as pl
from jax.experimental.pallas import tpu as pltpu
from jax.sharding import PartitionSpec as P

KAPPA = 0.16
LAMBDA = 0.015
EPS = 0.75

MESH = pl.DeviceIdType.MESH
SLOTS = 4
ROWS = 32
PAD = 4
ALL = ROWS + 2 * PAD
SIDE = 256
LANES = 128
PAIRS = 4
CHUNKS = 16
LAG = 3
MESSAGES = CHUNKS + LAG


def kernel(field, momenta, counts, accept, out, own, send_up, send_down, from_below, from_above, phi0, phi1, phi2, phi3, mom, moves, moves_at_ends, sides,
           done, turned, fields, slab, edges, flag, flags, a_ss, a_rs, c_ss, c_rs, ch_ss, ch_rs, f_ss, f_rs, up_ss, up_rs, down_ss, down_rs, z_ss, z_rs, zm_ss, zm_rs,
           r_ss, r_rs, d_ss, d_rs, e_ss, e_rs, here, home):
    rep, gz = lax.axis_index("rep"), lax.axis_index("gz")
    y, z = rep // 4, gz // 2
    q = (gz % 2) * 4 + rep % 4
    slot, half = rep % 4, gz % 2

    inner = pl.ds(0, ROWS)
    first, last = pl.ds(0, PAD), pl.ds(ROWS - PAD, PAD)
    high, low = pl.ds(ROWS, PAD), pl.ds(ROWS + PAD, PAD)
    beside_inner = pl.ds(ROWS, 2 * PAD)

    def place(ring, row, depth):
        return (row * 4 + ring % 4, depth * 2 + ring // 4)

    def ring(step):
        return place((q + step + 8) % 8, y, z)

    above, below = place(q, (y + 1) % 4, z), place(q, (y + 3) % 4, z)
    z_next, z_last = place(q, y, (z + 1) % 8), place(q, y, (z + 7) % 8)

    def remote(src, dst, ss, rs, device):
        return pltpu.make_async_remote_copy(src_ref=src, dst_ref=dst, send_sem=ss, recv_sem=rs, device_id=device, device_id_type=MESH)

    loads = [[], []]
    for n, (src, dst) in enumerate(((field, fields), (momenta, slab))):
        for side in range(2):
            loads[n].append(pltpu.make_async_copy(src.at[0, :, :, pl.ds(side * LANES, LANES)], dst.at[:, side], here.at[n, side]))
            loads[n][side].start()

    barrier = pltpu.get_barrier_semaphore()
    partners = [ring(step) for step in range(1, 8)] + [above, below, z_next, z_last]
    for device in partners:
        pl.semaphore_signal(barrier, inc=1, device_id=device, device_id_type=MESH)
    pl.semaphore_wait(barrier, len(partners))

    def rows_of(place_):
        return pl.ds(pl.multiple_of(place_ * ROWS, ROWS), ROWS)

    def local_plane(pair):
        return pair + half * (3 - 2 * pair)

    def field_copy(pair, step):
        src = fields.at[local_plane(pair), :, rows_of((q + step) % 8)]
        dst = own.at[pair, half, slot]
        if step == 0:
            return pltpu.make_async_copy(src, dst, a_rs.at[pair, 0])
        return remote(src, dst, a_ss.at[pair, step], a_rs.at[pair, step], ring(step))

    def momenta_copy(pair, step):
        src = slab.at[local_plane(pair), :, rows_of((q + step) % 8)]
        dst = mom.at[slot, 4 + half * 4 + local_plane(pair), :, inner]
        if step == 0:
            return pltpu.make_async_copy(src, dst, c_rs.at[pair, 0])
        return remote(src, dst, c_ss.at[pair, step], c_rs.at[pair, step], ring(step))

    def edge_copy(step):
        src, dst = edges.at[step], mom.at[slot, pl.ds(4 + half * 4, 4), :, beside_inner]
        if step == 0:
            return pltpu.make_async_copy(src, dst, ch_rs.at[0])
        return remote(src, dst, ch_ss.at[step], ch_rs.at[step], ring(step))

    def fill_edges():
        upper = lax.broadcasted_iota(jnp.int32, (2, 8, LANES), 1) < PAD
        for step in range(8):
            base = ((q + step) % 8) * ROWS
            after = pl.ds(pl.multiple_of((base + ROWS) % SIDE, 8), 8)
            ahead = pl.ds(pl.multiple_of((base + SIDE - 8) % SIDE, 8), 8)
            for plane in range(4):
                edges[step, plane] = jnp.where(upper, slab[plane, :, after, :], slab[plane, :, ahead, :])

    def flag_copy(step):
        if step == 0:
            return pltpu.make_async_copy(flag, flags.at[q], f_rs.at[0])
        return remote(flag, flags.at[q], f_ss.at[step], f_rs.at[step], ring(step))

    for load in loads[0]:
        load.wait()
    for step in range(8):
        field_copy(0, step).start()
    flag[...] = jnp.full(flag.shape, accept[0], jnp.int32)
    for step in range(8):
        flag_copy(step).start()

    alive = [[(counts[4 * ((y + d) % 4) + i] > 0).astype(jnp.int32) for i in range(4)] for d in range(4)]
    before = [[sum(alive[d][:i], jnp.int32(0)) for i in range(4)] for d in range(4)]
    total = [sum(alive[d], jnp.int32(0)) for d in range(4)]
    mine = [jnp.int32(-1)] * 4
    for c in range(4):
        for i in range(4):
            mine[c] = jnp.where((alive[0][i] == 1) & (before[0][i] == c), i, mine[c])
    split_up = jnp.minimum(total[3], 4 - total[2])
    split = jnp.minimum(total[2], 4 - total[1])
    cum, parent = jnp.int32(0), [jnp.int32(0)] * SLOTS
    for r in range(16):
        cum = cum + counts[r]
        for s in range(SLOTS):
            parent[s] = parent[s] + (cum <= 4 * y + s).astype(jnp.int32)
    code = []
    for s in range(SLOTS):
        value = jnp.int32(0)
        for d in range(4):
            for i in range(4):
                k = before[d][i]
                if d == 0:
                    way = jnp.int32(i)
                elif d == 1:
                    way = 4 + k
                elif d == 3:
                    way = 8 + k
                else:
                    way = jnp.where(k < split, 12 + total[1] + k, 16 + total[3] + k - split)
                value = jnp.where(parent[s] == 4 * ((y + d) % 4) + i, way, value)
        code.append(value)

    def same(value, number):
        return jnp.full((2, 8, LANES), value, jnp.int32) == number

    def octet(t):
        return t // 4, pl.ds(pl.multiple_of((t % 4) * 8, 8), 8)

    def assemble(t, forward):
        pair, rows = octet(jnp.minimum(t, CHUNKS - 1))
        for c in range(4):
            own_here = [same(mine[c], i) for i in range(4)]
            down_here = [same(total[0], c - f) for f in range(c + 1)]
            up_here = [same(split_up + c - total[0], f) for f in range(4)]
            for h in range(2):
                pieces = [own[pair, h, i, :, rows, :] for i in range(4)]
                if forward:
                    down, up = from_above[t - LAG, 0, h], from_below[t - LAG, 0, h]
                    for f in range(1, c + 1):
                        down = jnp.where(down_here[f], from_above[t - LAG, f, h], down)
                    for f in range(1, 4):
                        up = jnp.where(up_here[f], from_below[t - LAG, f, h], up)
                else:
                    down = up = pieces[0]
                for i in range(4):
                    down = jnp.where(own_here[i], pieces[i], down)
                    up = jnp.where(own_here[i], pieces[i], up)
                send_down[t, c, h] = down
                send_up[t, c, h] = up

    def up_copy(t):
        return remote(send_up.at[t], from_below.at[t], up_ss.at[t], up_rs.at[t], above)

    def down_copy(t):
        return remote(send_down.at[t], from_above.at[t], down_ss.at[t], down_rs.at[t], below)

    def pick(u):
        pair, rows = octet(u)
        for s in range(SLOTS):
            here_ = [same(code[s], k) for k in range(20)]
            for h in range(2):
                value = own[pair, h, 0, :, rows, :]
                for i in range(1, 4):
                    value = jnp.where(here_[i], own[pair, h, i, :, rows, :], value)
                for c in range(4):
                    value = jnp.where(here_[4 + c], from_above[u, c, h], value)
                    value = jnp.where(here_[8 + c], from_below[u, c, h], value)
                    value = jnp.where(here_[12 + c], from_above[u + LAG, c, h], value)
                    value = jnp.where(here_[16 + c], from_below[u + LAG, c, h], value)
                plane = 4 + pair if h == 0 else 11 - pair
                phi0[s, plane, :, rows, :] = value

    def z_copies(pair):
        return (
            remote(phi0.at[:, 4 + pair], phi0.at[:, 12 + pair], z_ss.at[pair, 0], z_rs.at[pair, 0], z_last),
            remote(phi0.at[:, 11 - pair], phi0.at[:, 3 - pair], z_ss.at[pair, 1], z_rs.at[pair, 1], z_next),
        )

    def zm_copies(pair):
        return (
            remote(mom.at[:, 4 + pair], mom.at[:, 12 + pair], zm_ss.at[pair, 0], zm_rs.at[pair, 0], z_last),
            remote(mom.at[:, 11 - pair], mom.at[:, 3 - pair], zm_ss.at[pair, 1], zm_rs.at[pair, 1], z_next),
        )

    def row_copies(pair):
        copies = []
        for n, plane in enumerate((4 + pair, 11 - pair)):
            copies.append(remote(phi0.at[:, plane, :, first], phi0.at[:, plane, :, high], r_ss.at[pair, n, 0], r_rs.at[pair, n, 0], ring(-1)))
            copies.append(remote(phi0.at[:, plane, :, last], phi0.at[:, plane, :, low], r_ss.at[pair, n, 1], r_rs.at[pair, n, 1], ring(1)))
        return copies

    def tick(t, carry):
        @pl.when(t < 3)
        def _():
            for step in range(8):
                field_copy(t + 1, step).start()

        @pl.when((t % 4 == 0) & (t < CHUNKS))
        def _():
            for step in range(8):
                copy = field_copy(t // 4, step)
                copy.wait() if step == 0 else copy.wait_recv()

        @pl.when(t >= LAG)
        def _():
            up_copy(t - LAG).wait_recv()
            down_copy(t - LAG).wait_recv()

        @pl.when(t < LAG)
        def _():
            assemble(t, False)

        @pl.when((t >= LAG) & (t < MESSAGES))
        def _():
            assemble(t, True)

        @pl.when(t < MESSAGES)
        def _():
            up_copy(t).start()
            down_copy(t).start()

        @pl.when(t == 4)
        def _():
            for load in loads[1]:
                load.wait()
            fill_edges()
            for step in range(8):
                edge_copy(step).start()

        @pl.when((t >= 6) & (t < 14) & (t % 2 == 0))
        def _():
            for step in range(8):
                momenta_copy((t - 6) // 2, step).start()

        @pl.when(t >= 2 * LAG)
        def _():
            pick(t - 2 * LAG)

        @pl.when((t >= 2 * LAG + 3) & ((t - 2 * LAG) % 4 == 3))
        def _():
            for copy in row_copies((t - 2 * LAG - 3) // 4):
                copy.start()

        @pl.when((t == 2 * LAG + 5) | (t == 2 * LAG + 9) | (t == 2 * LAG + 13))
        def _():
            pair = (t - 2 * LAG - 5) // 4
            for copy in row_copies(pair):
                copy.wait_recv()
            for copy in z_copies(pair):
                copy.start()

        @pl.when(t == 12)
        def _():
            for step in range(8):
                copy = edge_copy(step)
                copy.wait() if step == 0 else copy.wait_recv()

        @pl.when((t == 12) | (t == 14))
        def _():
            pair = (t - 12) // 2
            for step in range(8):
                copy = momenta_copy(pair, step)
                copy.wait() if step == 0 else copy.wait_recv()
            for copy in zm_copies(pair):
                copy.start()

        return carry

    lax.fori_loop(0, MESSAGES + LAG, tick, 0)

    for pair in range(2, PAIRS):
        for step in range(8):
            copy = momenta_copy(pair, step)
            copy.wait() if step == 0 else copy.wait_recv()
    for step in range(8):
        copy = flag_copy(step)
        copy.wait() if step == 0 else copy.wait_recv()
    for pair in range(2):
        for copy in zm_copies(pair):
            copy.wait()
    for pair in range(3):
        for copy in z_copies(pair):
            copy.wait_recv()
    for copy in row_copies(3):
        copy.wait_recv()

    def last_copies(s):
        return (
            remote(phi3.at[s, 0], sides.at[s, 1], d_ss.at[s, 0], d_rs.at[s, 0], z_last),
            remote(phi3.at[s, 7], sides.at[s, 0], d_ss.at[s, 1], d_rs.at[s, 1], z_next),
        )

    def result_copy(s, h, part, away):
        if part == 0:
            here_, there = pl.ds(1 + 3 * h, 3), pl.ds(1 - h, 3)
        else:
            here_, there = pl.ds(7 * h, 1), pl.ds(3 * h, 1)
        src, dst = done.at[s, here_], out.at[0, there, rows_of(q)]
        if away:
            return remote(src, dst, e_ss.at[s, h, part], e_rs.at[part, q], place(4 * h + s, y, z))
        return pltpu.make_async_copy(src, dst, home.at[part])

    def results(s, part, act):
        for h in range(2):
            @pl.when(q == 4 * h + s)
            def _():
                act(result_copy(s, h, part, False), False)

            @pl.when(q != 4 * h + s)
            def _():
                act(result_copy(s, h, part, True), True)

    tiles = range(ALL // 8)

    def spread(t):
        return pl.ds(t, 8, stride=ALL // 8)

    edge_lane = lax.broadcasted_iota(jnp.int32, (8, LANES), 1)
    first_lane, last_lane = edge_lane == 0, edge_lane == LANES - 1

    def natural(ref, plane):
        return [[ref[plane, n, spread(t), :] for t in tiles] for n in range(2)]

    def packed(ref, plane):
        return [[ref[plane, n, 8 * t:8 * t + 8, :] for t in tiles] for n in range(2)]

    def keep(ref, plane, values):
        for n in range(2):
            for t in tiles:
                ref[plane, n, 8 * t:8 * t + 8, :] = values[n][t]

    def each(act, *args):
        return [[act(*(arg[n][t] for arg in args)) for t in tiles] for n in range(2)]

    def kick(below_, centre, above_, scale):
        back = [[pltpu.roll(centre[n][t], 1, 1) for t in tiles] for n in range(2)]
        fore = [[pltpu.roll(centre[n][t], LANES - 1, 1) for t in tiles] for n in range(2)]
        result = [[], []]
        for n in range(2):
            for t in tiles:
                c = centre[n][t]
                ahead = centre[n][t - 1] if t > 0 else pltpu.roll(centre[n][-1], 1, 0)
                after = centre[n][t + 1] if t < len(tiles) - 1 else pltpu.roll(centre[n][0], 7, 0)
                left_ = jnp.where(first_lane, back[1 - n][t], back[n][t])
                right_ = jnp.where(last_lane, fore[1 - n][t], fore[n][t])
                beside = (below_[n][t] + above_[n][t]) + (ahead + after) + (left_ + right_)
                result[n].append((scale * 2.0 * KAPPA) * beside + c * (scale * (4.0 * LAMBDA - 2.0) - (scale * 4.0 * LAMBDA) * (c * c)))
        return result

    def finish(s, taken, plane, trio, move):
        push = kick(*trio, EPS * EPS)
        start = natural(phi0.at[s], 4 + plane)
        value = each(lambda c, m, f, b: jnp.where(taken, c + (m + f), b), trio[1], move, push, start)
        for n in range(2):
            for t in tiles:
                turned[plane, n, spread(t), :] = value[n][t]
            done[s, plane, :, n * LANES:(n + 1) * LANES] = turned[plane, n, :ROWS, :]

    def one_slot(n, carry):
        s = (n % 2) * 2 + n // 2
        taken = flags[s] == 1
        start = phi0.at[s]
        trio = [None, natural(start, 1), natural(start, 2)]
        for plane in range(2, 14):
            trio = trio[1:] + [natural(start, plane + 1)]
            move, push = natural(mom.at[s], plane), kick(*trio, 0.5 * EPS * EPS)
            move = each(lambda m, f: EPS * m + f, move, push)
            keep(moves, plane, move)
            keep(phi1, plane, each(lambda c, m: c + m, trio[1], move))
        for k, source, target in ((2, phi1, phi2), (3, phi2, phi3.at[s])):
            trio = [None, packed(source, k), packed(source, k + 1)]
            for plane in range(k + 1, 15 - k):
                trio = trio[1:] + [packed(source, plane + 1)]
                move, push = packed(moves, plane), kick(*trio, EPS * EPS)
                move = each(lambda m, f: m + f, move, push)
                if k == 3 and plane in (4, 11):
                    keep(moves_at_ends.at[s], plane // 11, move)
                else:
                    keep(moves, plane, move)
                keep(target, plane - (4 if k == 3 else 0), each(lambda c, m: c + m, trio[1], move))
        for copy in last_copies(s):
            copy.start()
        mine_ = phi3.at[s]
        trio = [None, packed(mine_, 0), packed(mine_, 1)]
        for plane in range(1, 7):
            trio = trio[1:] + [packed(mine_, plane + 1)]
            finish(s, taken, plane, trio, packed(moves, 4 + plane))
        results(s, 0, lambda copy, away: copy.start())
        return carry

    def both_ends(n, carry):
        s = (n % 2) * 2 + n // 2
        taken = flags[s] == 1
        for copy in last_copies(s):
            copy.wait_recv()
        mine_, beyond, held = phi3.at[s], sides.at[s], moves_at_ends.at[s]
        finish(s, taken, 0, [packed(beyond, 0), packed(mine_, 0), packed(mine_, 1)], packed(held, 0))
        finish(s, taken, 7, [packed(mine_, 6), packed(mine_, 7), packed(beyond, 1)], packed(held, 1))
        results(s, 1, lambda copy, away: copy.start())
        return carry

    lax.fori_loop(0, SLOTS, one_slot, 0)
    lax.fori_loop(0, SLOTS, both_ends, 0)

    for pair in range(PAIRS):
        for step in range(1, 8):
            field_copy(pair, step).wait_send()
            momenta_copy(pair, step).wait_send()
        for copy in row_copies(pair):
            copy.wait_send()
    for pair in range(3):
        for copy in z_copies(pair):
            copy.wait_send()
    for step in range(1, 8):
        flag_copy(step).wait_send()
        edge_copy(step).wait_send()

    def left(t, carry):
        up_copy(t).wait_send()
        down_copy(t).wait_send()
        return carry

    lax.fori_loop(0, MESSAGES, left, 0)
    for s in range(SLOTS):
        for copy in last_copies(s):
            copy.wait_send()
        for part in range(2):
            results(s, part, lambda copy, away: copy.wait_send() if away else copy.wait())
    for part in range(2):
        for step in range(1, 8):
            origin = (q + 8 - step) % 8
            size = pl.ds(0, 3 if part == 0 else 1)
            remote(done.at[0, size], out.at[0, size, rows_of(origin)], e_ss.at[0, 0, 0], e_rs.at[part, origin], ring(step)).wait_recv()


def local(field, momenta, counts, accept):
    f32, dma = jnp.float32, pltpu.SemaphoreType.DMA
    message = (MESSAGES, 4, 2, 2, 8, LANES)
    plane = (2, ALL, LANES)
    return pl.pallas_call(
        kernel,
        out_shape=jax.ShapeDtypeStruct(field.shape, f32),
        in_specs=[
            pl.BlockSpec(memory_space=pltpu.HBM),
            pl.BlockSpec(memory_space=pltpu.HBM),
            pl.BlockSpec(memory_space=pltpu.SMEM),
            pl.BlockSpec(memory_space=pltpu.SMEM),
        ],
        out_specs=pl.BlockSpec(memory_space=pl.ANY),
        scratch_shapes=[
            pltpu.VMEM((PAIRS, 2, SLOTS, 2, ROWS, LANES), f32),
            pltpu.VMEM(message, f32),
            pltpu.VMEM(message, f32),
            pltpu.VMEM(message, f32),
            pltpu.VMEM(message, f32),
            pltpu.VMEM((SLOTS, 16) + plane, f32),
            pltpu.VMEM((16,) + plane, f32),
            pltpu.VMEM((16,) + plane, f32),
            pltpu.VMEM((SLOTS, 8) + plane, f32),
            pltpu.VMEM((SLOTS, 16) + plane, f32),
            pltpu.VMEM((16,) + plane, f32),
            pltpu.VMEM((SLOTS, 2) + plane, f32),
            pltpu.VMEM((SLOTS, 2) + plane, f32),
            pltpu.VMEM((SLOTS, 8, ROWS, SIDE), f32),
            pltpu.VMEM((8,) + plane, f32),
            pltpu.VMEM((4, 2, SIDE, LANES), f32),
            pltpu.VMEM((4, 2, SIDE, LANES), f32),
            pltpu.VMEM((8, 4, 2, 8, LANES), f32),
            pltpu.VMEM((8, LANES), jnp.int32),
            pltpu.VMEM((8, 8, LANES), jnp.int32),
            dma((PAIRS, 8)), dma((PAIRS, 8)), dma((PAIRS, 8)), dma((PAIRS, 8)), dma((8,)), dma((8,)), dma((8,)), dma((8,)),
            dma((MESSAGES,)), dma((MESSAGES,)), dma((MESSAGES,)), dma((MESSAGES,)),
            dma((3, 2)), dma((3, 2)), dma((2, 2)), dma((2, 2)),
            dma((PAIRS, 2, 2)), dma((PAIRS, 2, 2)), dma((SLOTS, 2)), dma((SLOTS, 2)), dma((SLOTS, 2, 2)), dma((2, 8)), dma((2, 2)), dma((2,)),
        ],
        compiler_params=pltpu.CompilerParams(collective_id=0, has_side_effects=True, vmem_limit_bytes=60 * 1024 * 1024),
    )(field, momenta, counts, accept)


def solution(mesh):
    placed = (P("rep", "gz", None, None), P("rep", "gz", None, None), P(), P("rep"))
    return jax.shard_map(
        local, mesh=mesh, in_specs=placed, out_specs=P("rep", "gz", None, None), check_vma=False
    )
```

time: 82.9 us -> 73.9 us (0.89)
  Pallas kernels: 79.2 us -> 70.8 us
    pallas_call x1, Pallas kernels: 79.2 us -> 70.8 us  [local(): pl.pallas_call(kernel, out_shape=jax.ShapeDtypeStruct(field.shape, f32),...]
where the time goes in v3:
time: 73.9 us; the launch traced here: 73.7 us
  Pallas kernels  70.8 us (96%)
  local copies, waits for them, and re-layouts  2.29 us (3%)
    pallas_call x1, Pallas kernels, local(): pl.pallas_call(kernel, out_shape=jax.ShapeDtypeStruct(field.shape, f32),...  70.8 us
    unnamed x1, local copies, waits for them, and re-layouts  2.29 us

profile of v3, /device:TPU:1, one launch (start us, length us, event | category | flops | bytes accessed | tf_op | source)
XLA Modules:
  0.0 73.7 jit_solution(14998594525703035519)
XLA Ops:
  0.7 70.8 %shard_map.46 = f32[1,4,256,256]{3,2,1,0:T(8,128)} custom-call(f32[1,4,256,256]{3,2,1,0:T(8,128)} %field.1, f32[1,4,256,256]{3,2,1,0:T(8,128)} %momenta.1, s32[16]{0:T(128)} %counts.1, s32[1]{0:T(128)S(6)} %copy.6.accept), custom_call_target="tpu_custom_call" | custom-call | tf_op jit(solution)/shard_map/pallas_call | solution.py:458
  71.4 2.3 %copy.7 = f32[1,4,256,256]{3,2,1,0:T(8,128)} copy(f32[1,4,256,256]{3,2,1,0:T(8,128)} %shard_map.46) | data formatting | bytes 2097152

commit v4 on v3

--- a/solution.py
+++ b/solution.py
@@ -22,7 +22,7 @@
 MESSAGES = CHUNKS + LAG
 
 
-def kernel(field, momenta, counts, accept, out, own, send_up, send_down, from_below, from_above, phi0, phi1, phi2, phi3, mom, moves, moves_at_ends, sides,
+def kernel(field, momenta, counts, accept, out, own, send_up, send_down, from_below, from_above, phi0, phi1, phi2, phi3, mom, moves, sides,
            done, turned, fields, slab, edges, flag, flags, a_ss, a_rs, c_ss, c_rs, ch_ss, ch_rs, f_ss, f_rs, up_ss, up_rs, down_ss, down_rs, z_ss, z_rs, zm_ss, zm_rs,
            r_ss, r_rs, d_ss, d_rs, e_ss, e_rs, here, home):
     rep, gz = lax.axis_index("rep"), lax.axis_index("gz")
@@ -142,7 +142,8 @@
         return jnp.full((2, 8, LANES), value, jnp.int32) == number
 
     def octet(t):
-        return t // 4, pl.ds(pl.multiple_of((t % 4) * 8, 8), 8)
+        turn = t % 4
+        return t // 4, pl.ds(pl.multiple_of(jnp.where(turn == 0, 0, jnp.where(turn == 1, 24, turn * 8 - 8)), 8), 8)
 
     def assemble(t, forward):
         pair, rows = octet(jnp.minimum(t, CHUNKS - 1))
@@ -194,11 +195,10 @@
             remote(phi0.at[:, 11 - pair], phi0.at[:, 3 - pair], z_ss.at[pair, 1], z_rs.at[pair, 1], z_next),
         )
 
-    def zm_copies(pair):
-        return (
-            remote(mom.at[:, 4 + pair], mom.at[:, 12 + pair], zm_ss.at[pair, 0], zm_rs.at[pair, 0], z_last),
-            remote(mom.at[:, 11 - pair], mom.at[:, 3 - pair], zm_ss.at[pair, 1], zm_rs.at[pair, 1], z_next),
-        )
+    zm_copies = (
+        remote(mom.at[:, 4], mom.at[:, 12], zm_ss.at[0], zm_rs.at[0], z_last),
+        remote(mom.at[:, 11], mom.at[:, 3], zm_ss.at[1], zm_rs.at[1], z_next),
+    )
 
     def row_copies(pair):
         copies = []
@@ -254,14 +254,14 @@
         def _():
             pick(t - 2 * LAG)
 
-        @pl.when((t >= 2 * LAG + 3) & ((t - 2 * LAG) % 4 == 3))
-        def _():
-            for copy in row_copies((t - 2 * LAG - 3) // 4):
+        @pl.when((t >= 2 * LAG + 1) & ((t - 2 * LAG) % 4 == 1))
+        def _():
+            for copy in row_copies((t - 2 * LAG - 1) // 4):
                 copy.start()
 
-        @pl.when((t == 2 * LAG + 5) | (t == 2 * LAG + 9) | (t == 2 * LAG + 13))
-        def _():
-            pair = (t - 2 * LAG - 5) // 4
+        @pl.when((t == 2 * LAG + 3) | (t == 2 * LAG + 7))
+        def _():
+            pair = (t - 2 * LAG - 3) // 4
             for copy in row_copies(pair):
                 copy.wait_recv()
             for copy in z_copies(pair):
@@ -270,50 +270,43 @@
         @pl.when(t == 12)
         def _():
             for step in range(8):
-                copy = edge_copy(step)
-                copy.wait() if step == 0 else copy.wait_recv()
-
-        @pl.when((t == 12) | (t == 14))
-        def _():
-            pair = (t - 12) // 2
-            for step in range(8):
-                copy = momenta_copy(pair, step)
-                copy.wait() if step == 0 else copy.wait_recv()
-            for copy in zm_copies(pair):
+                for copy in (edge_copy(step), momenta_copy(0, step)):
+                    copy.wait() if step == 0 else copy.wait_recv()
+            for copy in zm_copies:
                 copy.start()
 
         return carry
 
     lax.fori_loop(0, MESSAGES + LAG, tick, 0)
 
-    for pair in range(2, PAIRS):
+    for pair in range(1, PAIRS):
         for step in range(8):
             copy = momenta_copy(pair, step)
             copy.wait() if step == 0 else copy.wait_recv()
     for step in range(8):
         copy = flag_copy(step)
         copy.wait() if step == 0 else copy.wait_recv()
+    for copy in zm_copies:
+        copy.wait()
     for pair in range(2):
-        for copy in zm_copies(pair):
-            copy.wait()
-    for pair in range(3):
         for copy in z_copies(pair):
             copy.wait_recv()
-    for copy in row_copies(3):
+    for copy in row_copies(2) + row_copies(3):
         copy.wait_recv()
 
-    def last_copies(s):
+    def end_copies(k, s):
+        src, n = (phi2, phi3)[k - 2].at[s], k - 2
         return (
-            remote(phi3.at[s, 0], sides.at[s, 1], d_ss.at[s, 0], d_rs.at[s, 0], z_last),
-            remote(phi3.at[s, 7], sides.at[s, 0], d_ss.at[s, 1], d_rs.at[s, 1], z_next),
+            remote(src.at[0], sides.at[n, s, 1], d_ss.at[n, s, 0], d_rs.at[n, s, 0], z_last),
+            remote(src.at[7], sides.at[n, s, 0], d_ss.at[n, s, 1], d_rs.at[n, s, 1], z_next),
         )
 
+    PARTS = ((2, 2), (1, 1), (0, 1))
+
     def result_copy(s, h, part, away):
-        if part == 0:
-            here_, there = pl.ds(1 + 3 * h, 3), pl.ds(1 - h, 3)
-        else:
-            here_, there = pl.ds(7 * h, 1), pl.ds(3 * h, 1)
-        src, dst = done.at[s, here_], out.at[0, there, rows_of(q)]
+        first_plane, number = PARTS[part]
+        src = done.at[s, pl.ds(8 - number - first_plane if h else first_plane, number)]
+        dst = out.at[0, pl.ds(4 - number - first_plane if h else first_plane, number), rows_of(q)]
         if away:
             return remote(src, dst, e_ss.at[s, h, part], e_rs.at[part, q], place(4 * h + s, y, z))
         return pltpu.make_async_copy(src, dst, home.at[part])
@@ -374,51 +367,77 @@
                 turned[plane, n, spread(t), :] = value[n][t]
             done[s, plane, :, n * LANES:(n + 1) * LANES] = turned[plane, n, :ROWS, :]
 
+    def advance(trio, move, scale=EPS * EPS):
+        push = kick(*trio, scale)
+        move = each(lambda m, f: m + f, move, push)
+        return move, each(lambda c, m: c + m, trio[1], move)
+
     def one_slot(n, carry):
         s = (n % 2) * 2 + n // 2
         taken = flags[s] == 1
-        start = phi0.at[s]
-        trio = [None, natural(start, 1), natural(start, 2)]
-        for plane in range(2, 14):
+        start, second, third, held = phi0.at[s], phi2.at[s], phi3.at[s], moves.at[s]
+        trio = [None, natural(start, 2), natural(start, 3)]
+        for plane in range(3, 13):
             trio = trio[1:] + [natural(start, plane + 1)]
-            move, push = natural(mom.at[s], plane), kick(*trio, 0.5 * EPS * EPS)
-            move = each(lambda m, f: EPS * m + f, move, push)
-            keep(moves, plane, move)
-            keep(phi1, plane, each(lambda c, m: c + m, trio[1], move))
-        for k, source, target in ((2, phi1, phi2), (3, phi2, phi3.at[s])):
-            trio = [None, packed(source, k), packed(source, k + 1)]
-            for plane in range(k + 1, 15 - k):
-                trio = trio[1:] + [packed(source, plane + 1)]
-                move, push = packed(moves, plane), kick(*trio, EPS * EPS)
-                move = each(lambda m, f: m + f, move, push)
-                if k == 3 and plane in (4, 11):
-                    keep(moves_at_ends.at[s], plane // 11, move)
-                else:
-                    keep(moves, plane, move)
-                keep(target, plane - (4 if k == 3 else 0), each(lambda c, m: c + m, trio[1], move))
-        for copy in last_copies(s):
+            move = each(lambda m: EPS * m, natural(mom.at[s], plane))
+            move, value = advance(trio, move, 0.5 * EPS * EPS)
+            if 4 <= plane < 12:
+                keep(held, plane - 4, move)
+            keep(phi1, plane - 3, value)
+        trio = [None, packed(phi1, 0), packed(phi1, 1)]
+        for plane in range(8):
+            trio = trio[1:] + [packed(phi1, plane + 2)]
+            move, value = advance(trio, packed(held, plane))
+            keep(held, plane, move)
+            keep(second, plane, value)
+        for copy in end_copies(2, s):
             copy.start()
-        mine_ = phi3.at[s]
-        trio = [None, packed(mine_, 0), packed(mine_, 1)]
+        trio = [None, packed(second, 0), packed(second, 1)]
         for plane in range(1, 7):
-            trio = trio[1:] + [packed(mine_, plane + 1)]
-            finish(s, taken, plane, trio, packed(moves, 4 + plane))
+            trio = trio[1:] + [packed(second, plane + 1)]
+            move, value = advance(trio, packed(held, plane))
+            keep(held, plane, move)
+            keep(third, plane, value)
+        trio = [None, packed(third, 1), packed(third, 2)]
+        for plane in range(2, 6):
+            trio = trio[1:] + [packed(third, plane + 1)]
+            finish(s, taken, plane, trio, packed(held, plane))
         results(s, 0, lambda copy, away: copy.start())
         return carry
 
-    def both_ends(n, carry):
+    def next_planes(n, carry):
         s = (n % 2) * 2 + n // 2
         taken = flags[s] == 1
-        for copy in last_copies(s):
+        second, third, held, beyond = phi2.at[s], phi3.at[s], moves.at[s], sides.at[0, s]
+        for copy in end_copies(2, s):
             copy.wait_recv()
-        mine_, beyond, held = phi3.at[s], sides.at[s], moves_at_ends.at[s]
-        finish(s, taken, 0, [packed(beyond, 0), packed(mine_, 0), packed(mine_, 1)], packed(held, 0))
-        finish(s, taken, 7, [packed(mine_, 6), packed(mine_, 7), packed(beyond, 1)], packed(held, 1))
+        for plane in (0, 7):
+            inside = packed(second, 1 if plane == 0 else 6)
+            move, value = advance([packed(beyond, plane // 7), packed(second, plane), inside], packed(held, plane))
+            keep(held, plane, move)
+            keep(third, plane, value)
+        for copy in end_copies(3, s):
+            copy.start()
+        for plane in (1, 6):
+            finish(s, taken, plane, [packed(third, plane + n_) for n_ in (-1, 0, 1)], packed(held, plane))
         results(s, 1, lambda copy, away: copy.start())
         return carry
 
+    def end_planes(n, carry):
+        s = (n % 2) * 2 + n // 2
+        taken = flags[s] == 1
+        third, held, beyond = phi3.at[s], moves.at[s], sides.at[1, s]
+        for copy in end_copies(3, s):
+            copy.wait_recv()
+        for plane in (0, 7):
+            inside = packed(third, 1 if plane == 0 else 6)
+            finish(s, taken, plane, [packed(beyond, plane // 7), packed(third, plane), inside], packed(held, plane))
+        results(s, 2, lambda copy, away: copy.start())
+        return carry
+
     lax.fori_loop(0, SLOTS, one_slot, 0)
-    lax.fori_loop(0, SLOTS, both_ends, 0)
+    lax.fori_loop(0, SLOTS, next_planes, 0)
+    lax.fori_loop(0, SLOTS, end_planes, 0)
 
     for pair in range(PAIRS):
         for step in range(1, 8):
@@ -426,7 +445,7 @@
             momenta_copy(pair, step).wait_send()
         for copy in row_copies(pair):
             copy.wait_send()
-    for pair in range(3):
+    for pair in range(2):
         for copy in z_copies(pair):
             copy.wait_send()
     for step in range(1, 8):
@@ -440,14 +459,14 @@
 
     lax.fori_loop(0, MESSAGES, left, 0)
     for s in range(SLOTS):
-        for copy in last_copies(s):
+        for copy in end_copies(2, s) + end_copies(3, s):
             copy.wait_send()
-        for part in range(2):
+        for part in range(3):
             results(s, part, lambda copy, away: copy.wait_send() if away else copy.wait())
-    for part in range(2):
+    for part in range(3):
         for step in range(1, 8):
             origin = (q + 8 - step) % 8
-            size = pl.ds(0, 3 if part == 0 else 1)
+            size = pl.ds(0, PARTS[part][1])
             remote(done.at[0, size], out.at[0, size, rows_of(origin)], e_ss.at[0, 0, 0], e_rs.at[part, origin], ring(step)).wait_recv()
 
 
@@ -464,7 +483,7 @@
             pl.BlockSpec(memory_space=pltpu.SMEM),
             pl.BlockSpec(memory_space=pltpu.SMEM),
         ],
-        out_specs=pl.BlockSpec(memory_space=pl.ANY),
+        out_specs=pl.BlockSpec(memory_space=pltpu.VMEM),
         scratch_shapes=[
             pltpu.VMEM((PAIRS, 2, SLOTS, 2, ROWS, LANES), f32),
             pltpu.VMEM(message, f32),
@@ -472,13 +491,12 @@
             pltpu.VMEM(message, f32),
             pltpu.VMEM(message, f32),
             pltpu.VMEM((SLOTS, 16) + plane, f32),
-            pltpu.VMEM((16,) + plane, f32),
-            pltpu.VMEM((16,) + plane, f32),
+            pltpu.VMEM((10,) + plane, f32),
+            pltpu.VMEM((SLOTS, 8) + plane, f32),
             pltpu.VMEM((SLOTS, 8) + plane, f32),
             pltpu.VMEM((SLOTS, 16) + plane, f32),
-            pltpu.VMEM((16,) + plane, f32),
-            pltpu.VMEM((SLOTS, 2) + plane, f32),
-            pltpu.VMEM((SLOTS, 2) + plane, f32),
+            pltpu.VMEM((SLOTS, 8) + plane, f32),
+            pltpu.VMEM((2, SLOTS, 2) + plane, f32),
             pltpu.VMEM((SLOTS, 8, ROWS, SIDE), f32),
             pltpu.VMEM((8,) + plane, f32),
             pltpu.VMEM((4, 2, SIDE, LANES), f32),
@@ -488,10 +506,10 @@
             pltpu.VMEM((8, 8, LANES), jnp.int32),
             dma((PAIRS, 8)), dma((PAIRS, 8)), dma((PAIRS, 8)), dma((PAIRS, 8)), dma((8,)), dma((8,)), dma((8,)), dma((8,)),
             dma((MESSAGES,)), dma((MESSAGES,)), dma((MESSAGES,)), dma((MESSAGES,)),
-            dma((3, 2)), dma((3, 2)), dma((2, 2)), dma((2, 2)),
-            dma((PAIRS, 2, 2)), dma((PAIRS, 2, 2)), dma((SLOTS, 2)), dma((SLOTS, 2)), dma((SLOTS, 2, 2)), dma((2, 8)), dma((2, 2)), dma((2,)),
+            dma((2, 2)), dma((2, 2)), dma((2,)), dma((2,)),
+            dma((PAIRS, 2, 2)), dma((PAIRS, 2, 2)), dma((2, SLOTS, 2)), dma((2, SLOTS, 2)), dma((SLOTS, 2, 3)), dma((3, 8)), dma((2, 2)), dma((3,)),
         ],
-        compiler_params=pltpu.CompilerParams(collective_id=0, has_side_effects=True, vmem_limit_bytes=60 * 1024 * 1024),
+        compiler_params=pltpu.CompilerParams(collective_id=0, has_side_effects=True, vmem_limit_bytes=52 * 1024 * 1024),
     )(field, momenta, counts, accept)
 
 

time: 73.9 us -> 65.4 us (0.88)
  Pallas kernels: 70.8 us -> 63.7 us
  local copies, waits for them, and re-layouts: 2.29 us -> 0.98 us
    pallas_call x1, Pallas kernels: 70.8 us -> 63.7 us  [local(): pl.pallas_call(kernel, out_shape=jax.ShapeDtypeStruct(field.shape, f32),...]
    unnamed x1 -> x3, local copies, waits for them, and re-layouts: 2.29 us -> 0.98 us
where the time goes in v4:
time: 65.4 us
  Pallas kernels  63.7 us (97%)
  local copies, waits for them, and re-layouts  0.98 us (1%)
  between operations  0.68 us (1%)
    pallas_call x1, Pallas kernels, local(): pl.pallas_call(kernel, out_shape=jax.ShapeDtypeStruct(field.shape, f32),...  63.7 us

profile of v4, /device:TPU:1, one launch (start us, length us, event | category | flops | bytes accessed | tf_op | source)
XLA Modules:
  0.0 65.4 jit_solution(1013428359484830702)
XLA Ops:
  0.0 0.0 copy-start
  0.7 0.0 copy-done
  0.7 63.7 %shard_map.46 = f32[1,4,256,256]{3,2,1,0:T(8,128)S(1)} custom-call(f32[1,4,256,256]{3,2,1,0:T(8,128)} %field.1, f32[1,4,256,256]{3,2,1,0:T(8,128)} %momenta.1, s32[16]{0:T(128)S(1)} %copy-done, s32[1]{0:T(128)S(6)} %copy.6.accept), custom_call_target="tpu_custom_call" | custom-call | tf_op jit(solution)/shard_map/pallas_call | solution.py:477
  64.4 1.0 %copy.7 = f32[1,4,256,256]{3,2,1,0:T(8,128)} copy(f32[1,4,256,256]{3,2,1,0:T(8,128)S(1)} %shard_map.46) | data formatting | bytes 2097152
Async XLA Ops:
  0.0 0.7 %copy-start = (s32[16]{0:T(128)S(1)}, s32[16]{0:T(128)}, u32[]{:S(2)}) copy-start(s32[16]{0:T(128)} %counts.1) | copy-start | bytes 196

commit v5 on v4

--- a/solution.py
+++ b/solution.py
@@ -24,7 +24,7 @@
 
 def kernel(field, momenta, counts, accept, out, own, send_up, send_down, from_below, from_above, phi0, phi1, phi2, phi3, mom, moves, sides,
            done, turned, fields, slab, edges, flag, flags, a_ss, a_rs, c_ss, c_rs, ch_ss, ch_rs, f_ss, f_rs, up_ss, up_rs, down_ss, down_rs, z_ss, z_rs, zm_ss, zm_rs,
-           r_ss, r_rs, d_ss, d_rs, e_ss, e_rs, here, home):
+           r_ss, r_rs, d_ss, d_rs, e_ss, e_rs, here):
     rep, gz = lax.axis_index("rep"), lax.axis_index("gz")
     y, z = rep // 4, gz // 2
     q = (gz % 2) * 4 + rep % 4
@@ -47,11 +47,12 @@
     def remote(src, dst, ss, rs, device):
         return pltpu.make_async_remote_copy(src_ref=src, dst_ref=dst, send_sem=ss, recv_sem=rs, device_id=device, device_id_type=MESH)
 
-    loads = [[], []]
+    def took(like, sem):
+        pltpu.make_async_copy(like, like, sem).wait()
+
     for n, (src, dst) in enumerate(((field, fields), (momenta, slab))):
         for side in range(2):
-            loads[n].append(pltpu.make_async_copy(src.at[0, :, :, pl.ds(side * LANES, LANES)], dst.at[:, side], here.at[n, side]))
-            loads[n][side].start()
+            pltpu.make_async_copy(src.at[0, :, :, pl.ds(side * LANES, LANES)], dst.at[:, side], here.at[n]).start()
 
     barrier = pltpu.get_barrier_semaphore()
     partners = [ring(step) for step in range(1, 8)] + [above, below, z_next, z_last]
@@ -69,21 +70,21 @@
         src = fields.at[local_plane(pair), :, rows_of((q + step) % 8)]
         dst = own.at[pair, half, slot]
         if step == 0:
-            return pltpu.make_async_copy(src, dst, a_rs.at[pair, 0])
-        return remote(src, dst, a_ss.at[pair, step], a_rs.at[pair, step], ring(step))
+            return pltpu.make_async_copy(src, dst, a_rs.at[pair])
+        return remote(src, dst, a_ss, a_rs.at[pair], ring(step))
 
     def momenta_copy(pair, step):
         src = slab.at[local_plane(pair), :, rows_of((q + step) % 8)]
         dst = mom.at[slot, 4 + half * 4 + local_plane(pair), :, inner]
         if step == 0:
-            return pltpu.make_async_copy(src, dst, c_rs.at[pair, 0])
-        return remote(src, dst, c_ss.at[pair, step], c_rs.at[pair, step], ring(step))
+            return pltpu.make_async_copy(src, dst, c_rs.at[pair])
+        return remote(src, dst, c_ss, c_rs.at[pair], ring(step))
 
     def edge_copy(step):
         src, dst = edges.at[step], mom.at[slot, pl.ds(4 + half * 4, 4), :, beside_inner]
         if step == 0:
-            return pltpu.make_async_copy(src, dst, ch_rs.at[0])
-        return remote(src, dst, ch_ss.at[step], ch_rs.at[step], ring(step))
+            return pltpu.make_async_copy(src, dst, ch_rs)
+        return remote(src, dst, ch_ss, ch_rs, ring(step))
 
     def fill_edges():
         upper = lax.broadcasted_iota(jnp.int32, (2, 8, LANES), 1) < PAD
@@ -96,16 +97,13 @@
 
     def flag_copy(step):
         if step == 0:
-            return pltpu.make_async_copy(flag, flags.at[q], f_rs.at[0])
-        return remote(flag, flags.at[q], f_ss.at[step], f_rs.at[step], ring(step))
-
-    for load in loads[0]:
-        load.wait()
+            return pltpu.make_async_copy(flag, flags.at[q], f_rs)
+        return remote(flag, flags.at[q], f_ss, f_rs, ring(step))
+
+    took(fields, here.at[0])
     for step in range(8):
         field_copy(0, step).start()
     flag[...] = jnp.full(flag.shape, accept[0], jnp.int32)
-    for step in range(8):
-        flag_copy(step).start()
 
     alive = [[(counts[4 * ((y + d) % 4) + i] > 0).astype(jnp.int32) for i in range(4)] for d in range(4)]
     before = [[sum(alive[d][:i], jnp.int32(0)) for i in range(4)] for d in range(4)]
@@ -168,10 +166,10 @@
                 send_up[t, c, h] = up
 
     def up_copy(t):
-        return remote(send_up.at[t], from_below.at[t], up_ss.at[t], up_rs.at[t], above)
+        return remote(send_up.at[t], from_below.at[t], up_ss, up_rs.at[t], above)
 
     def down_copy(t):
-        return remote(send_down.at[t], from_above.at[t], down_ss.at[t], down_rs.at[t], below)
+        return remote(send_down.at[t], from_above.at[t], down_ss, down_rs.at[t], below)
 
     def pick(u):
         pair, rows = octet(u)
@@ -191,21 +189,24 @@
 
     def z_copies(pair):
         return (
-            remote(phi0.at[:, 4 + pair], phi0.at[:, 12 + pair], z_ss.at[pair, 0], z_rs.at[pair, 0], z_last),
-            remote(phi0.at[:, 11 - pair], phi0.at[:, 3 - pair], z_ss.at[pair, 1], z_rs.at[pair, 1], z_next),
+            remote(phi0.at[:, 4 + pair], phi0.at[:, 12 + pair], z_ss, z_rs.at[pair], z_last),
+            remote(phi0.at[:, 11 - pair], phi0.at[:, 3 - pair], z_ss, z_rs.at[pair], z_next),
         )
 
     zm_copies = (
-        remote(mom.at[:, 4], mom.at[:, 12], zm_ss.at[0], zm_rs.at[0], z_last),
-        remote(mom.at[:, 11], mom.at[:, 3], zm_ss.at[1], zm_rs.at[1], z_next),
+        remote(mom.at[:, 4], mom.at[:, 12], zm_ss, zm_rs, z_last),
+        remote(mom.at[:, 11], mom.at[:, 3], zm_ss, zm_rs, z_next),
     )
 
     def row_copies(pair):
         copies = []
         for n, plane in enumerate((4 + pair, 11 - pair)):
-            copies.append(remote(phi0.at[:, plane, :, first], phi0.at[:, plane, :, high], r_ss.at[pair, n, 0], r_rs.at[pair, n, 0], ring(-1)))
-            copies.append(remote(phi0.at[:, plane, :, last], phi0.at[:, plane, :, low], r_ss.at[pair, n, 1], r_rs.at[pair, n, 1], ring(1)))
+            copies.append(remote(phi0.at[:, plane, :, first], phi0.at[:, plane, :, high], r_ss, r_rs.at[pair], ring(-1)))
+            copies.append(remote(phi0.at[:, plane, :, last], phi0.at[:, plane, :, low], r_ss, r_rs.at[pair], ring(1)))
         return copies
+
+    momenta_pair = mom.at[:, pl.ds(4, 2), :, inner]
+    row_halo = phi0.at[:, pl.ds(4, 2), :, beside_inner]
 
     def tick(t, carry):
         @pl.when(t < 3)
@@ -215,9 +216,7 @@
 
         @pl.when((t % 4 == 0) & (t < CHUNKS))
         def _():
-            for step in range(8):
-                copy = field_copy(t // 4, step)
-                copy.wait() if step == 0 else copy.wait_recv()
+            took(own.at[t // 4], a_rs.at[t // 4])
 
         @pl.when(t >= LAG)
         def _():
@@ -239,11 +238,11 @@
 
         @pl.when(t == 4)
         def _():
-            for load in loads[1]:
-                load.wait()
+            took(slab, here.at[1])
             fill_edges()
             for step in range(8):
                 edge_copy(step).start()
+                flag_copy(step).start()
 
         @pl.when((t >= 6) & (t < 14) & (t % 2 == 0))
         def _():
@@ -262,16 +261,14 @@
         @pl.when((t == 2 * LAG + 3) | (t == 2 * LAG + 7))
         def _():
             pair = (t - 2 * LAG - 3) // 4
-            for copy in row_copies(pair):
-                copy.wait_recv()
+            took(row_halo, r_rs.at[pair])
             for copy in z_copies(pair):
                 copy.start()
 
         @pl.when(t == 12)
         def _():
-            for step in range(8):
-                for copy in (edge_copy(step), momenta_copy(0, step)):
-                    copy.wait() if step == 0 else copy.wait_recv()
+            took(mom.at[:, pl.ds(4, 8), :, beside_inner], ch_rs)
+            took(momenta_pair, c_rs.at[0])
             for copy in zm_copies:
                 copy.start()
 
@@ -280,25 +277,20 @@
     lax.fori_loop(0, MESSAGES + LAG, tick, 0)
 
     for pair in range(1, PAIRS):
-        for step in range(8):
-            copy = momenta_copy(pair, step)
-            copy.wait() if step == 0 else copy.wait_recv()
-    for step in range(8):
-        copy = flag_copy(step)
-        copy.wait() if step == 0 else copy.wait_recv()
-    for copy in zm_copies:
-        copy.wait()
+        took(momenta_pair, c_rs.at[pair])
+    took(flags, f_rs)
+    took(mom.at[:, pl.ds(0, 2)], zm_rs)
+    took(mom.at[:, pl.ds(0, 2)], zm_ss)
     for pair in range(2):
-        for copy in z_copies(pair):
-            copy.wait_recv()
-    for copy in row_copies(2) + row_copies(3):
-        copy.wait_recv()
+        took(phi0.at[:, pl.ds(0, 2)], z_rs.at[pair])
+    for pair in range(2, PAIRS):
+        took(row_halo, r_rs.at[pair])
 
     def end_copies(k, s):
         src, n = (phi2, phi3)[k - 2].at[s], k - 2
         return (
-            remote(src.at[0], sides.at[n, s, 1], d_ss.at[n, s, 0], d_rs.at[n, s, 0], z_last),
-            remote(src.at[7], sides.at[n, s, 0], d_ss.at[n, s, 1], d_rs.at[n, s, 1], z_next),
+            remote(src.at[0], sides.at[n, s, 1], d_ss, d_rs.at[n, s], z_last),
+            remote(src.at[7], sides.at[n, s, 0], d_ss, d_rs.at[n, s], z_next),
         )
 
     PARTS = ((2, 2), (1, 1), (0, 1))
@@ -308,18 +300,18 @@
         src = done.at[s, pl.ds(8 - number - first_plane if h else first_plane, number)]
         dst = out.at[0, pl.ds(4 - number - first_plane if h else first_plane, number), rows_of(q)]
         if away:
-            return remote(src, dst, e_ss.at[s, h, part], e_rs.at[part, q], place(4 * h + s, y, z))
-        return pltpu.make_async_copy(src, dst, home.at[part])
-
-    def results(s, part, act):
+            return remote(src, dst, e_ss, e_rs, place(4 * h + s, y, z))
+        return pltpu.make_async_copy(src, dst, e_rs)
+
+    def results(s, part):
         for h in range(2):
             @pl.when(q == 4 * h + s)
             def _():
-                act(result_copy(s, h, part, False), False)
+                result_copy(s, h, part, False).start()
 
             @pl.when(q != 4 * h + s)
             def _():
-                act(result_copy(s, h, part, True), True)
+                result_copy(s, h, part, True).start()
 
     tiles = range(ALL // 8)
 
@@ -402,15 +394,14 @@
         for plane in range(2, 6):
             trio = trio[1:] + [packed(third, plane + 1)]
             finish(s, taken, plane, trio, packed(held, plane))
-        results(s, 0, lambda copy, away: copy.start())
+        results(s, 0)
         return carry
 
     def next_planes(n, carry):
         s = (n % 2) * 2 + n // 2
         taken = flags[s] == 1
         second, third, held, beyond = phi2.at[s], phi3.at[s], moves.at[s], sides.at[0, s]
-        for copy in end_copies(2, s):
-            copy.wait_recv()
+        took(sides.at[0, s], d_rs.at[0, s])
         for plane in (0, 7):
             inside = packed(second, 1 if plane == 0 else 6)
             move, value = advance([packed(beyond, plane // 7), packed(second, plane), inside], packed(held, plane))
@@ -420,54 +411,36 @@
             copy.start()
         for plane in (1, 6):
             finish(s, taken, plane, [packed(third, plane + n_) for n_ in (-1, 0, 1)], packed(held, plane))
-        results(s, 1, lambda copy, away: copy.start())
+        results(s, 1)
         return carry
 
     def end_planes(n, carry):
         s = (n % 2) * 2 + n // 2
         taken = flags[s] == 1
         third, held, beyond = phi3.at[s], moves.at[s], sides.at[1, s]
-        for copy in end_copies(3, s):
-            copy.wait_recv()
+        took(sides.at[1, s], d_rs.at[1, s])
         for plane in (0, 7):
             inside = packed(third, 1 if plane == 0 else 6)
             finish(s, taken, plane, [packed(beyond, plane // 7), packed(third, plane), inside], packed(held, plane))
-        results(s, 2, lambda copy, away: copy.start())
+        results(s, 2)
         return carry
 
     lax.fori_loop(0, SLOTS, one_slot, 0)
     lax.fori_loop(0, SLOTS, next_planes, 0)
     lax.fori_loop(0, SLOTS, end_planes, 0)
 
-    for pair in range(PAIRS):
-        for step in range(1, 8):
-            field_copy(pair, step).wait_send()
-            momenta_copy(pair, step).wait_send()
-        for copy in row_copies(pair):
-            copy.wait_send()
-    for pair in range(2):
-        for copy in z_copies(pair):
-            copy.wait_send()
-    for step in range(1, 8):
-        flag_copy(step).wait_send()
-        edge_copy(step).wait_send()
-
-    def left(t, carry):
-        up_copy(t).wait_send()
-        down_copy(t).wait_send()
-        return carry
-
-    lax.fori_loop(0, MESSAGES, left, 0)
-    for s in range(SLOTS):
-        for copy in end_copies(2, s) + end_copies(3, s):
-            copy.wait_send()
-        for part in range(3):
-            results(s, part, lambda copy, away: copy.wait_send() if away else copy.wait())
-    for part in range(3):
-        for step in range(1, 8):
-            origin = (q + 8 - step) % 8
-            size = pl.ds(0, PARTS[part][1])
-            remote(done.at[0, size], out.at[0, size, rows_of(origin)], e_ss.at[0, 0, 0], e_rs.at[part, origin], ring(step)).wait_recv()
+    seven = pl.ds(0, 7 * ROWS)
+    took(fields.at[:, :, seven], a_ss)
+    took(slab.at[:, :, seven], c_ss)
+    took(edges.at[pl.ds(0, 7)], ch_ss)
+    took(flags.at[pl.ds(0, 7)], f_ss)
+    took(send_up, up_ss)
+    took(send_down, down_ss)
+    took(phi0.at[:, pl.ds(0, 4)], z_ss)
+    took(phi0.at[:, pl.ds(4, 8), :, beside_inner], r_ss)
+    took(sides, d_ss)
+    took(out.at[0, :, seven], e_ss)
+    took(out, e_rs)
 
 
 def local(field, momenta, counts, accept):
@@ -504,10 +477,10 @@
             pltpu.VMEM((8, 4, 2, 8, LANES), f32),
             pltpu.VMEM((8, LANES), jnp.int32),
             pltpu.VMEM((8, 8, LANES), jnp.int32),
-            dma((PAIRS, 8)), dma((PAIRS, 8)), dma((PAIRS, 8)), dma((PAIRS, 8)), dma((8,)), dma((8,)), dma((8,)), dma((8,)),
-            dma((MESSAGES,)), dma((MESSAGES,)), dma((MESSAGES,)), dma((MESSAGES,)),
-            dma((2, 2)), dma((2, 2)), dma((2,)), dma((2,)),
-            dma((PAIRS, 2, 2)), dma((PAIRS, 2, 2)), dma((2, SLOTS, 2)), dma((2, SLOTS, 2)), dma((SLOTS, 2, 3)), dma((3, 8)), dma((2, 2)), dma((3,)),
+            dma, dma((PAIRS,)), dma, dma((PAIRS,)), dma, dma, dma, dma,
+            dma, dma((MESSAGES,)), dma, dma((MESSAGES,)),
+            dma, dma((2,)), dma, dma,
+            dma, dma((PAIRS,)), dma, dma((2, SLOTS)), dma, dma, dma((2,)),
         ],
         compiler_params=pltpu.CompilerParams(collective_id=0, has_side_effects=True, vmem_limit_bytes=52 * 1024 * 1024),
     )(field, momenta, counts, accept)

time: 65.4 us -> 63.5 us (0.971)
  Pallas kernels: 63.7 us -> 61.8 us
    pallas_call x1, Pallas kernels: 63.7 us -> 61.8 us  [local(): pl.pallas_call(kernel, out_shape=jax.ShapeDtypeStruct(field.shape, f32),...]
where the time goes in v5:
time: 63.5 us; the launch traced here: 63.4 us
  Pallas kernels  61.8 us (97%)
  local copies, waits for them, and re-layouts  0.98 us (2%)
  between operations  0.68 us (1%)
    pallas_call x1, Pallas kernels, local(): pl.pallas_call(kernel, out_shape=jax.ShapeDtypeStruct(field.shape, f32),...  61.8 us

profile of v5, /device:TPU:1, one launch (start us, length us, event | category | flops | bytes accessed | tf_op | source)
XLA Modules:
  0.0 63.4 jit_solution(5245258067315919358)
XLA Ops:
  0.0 0.0 copy-start
  0.7 0.0 copy-done
  0.7 61.8 %shard_map.46 = f32[1,4,256,256]{3,2,1,0:T(8,128)S(1)} custom-call(f32[1,4,256,256]{3,2,1,0:T(8,128)} %field.1, f32[1,4,256,256]{3,2,1,0:T(8,128)} %momenta.1, s32[16]{0:T(128)S(1)} %copy-done, s32[1]{0:T(128)S(6)} %copy.6.accept), custom_call_target="tpu_custom_call" | custom-call | tf_op jit(solution)/shard_map/pallas_call | solution.py:450
  62.5 1.0 %copy.7 = f32[1,4,256,256]{3,2,1,0:T(8,128)} copy(f32[1,4,256,256]{3,2,1,0:T(8,128)S(1)} %shard_map.46) | data formatting | bytes 2097152
Async XLA Ops:
  0.0 0.7 %copy-start = (s32[16]{0:T(128)S(1)}, s32[16]{0:T(128)}, u32[]{:S(2)}) copy-start(s32[16]{0:T(128)} %counts.1) | copy-start | bytes 196

commit v6 on v5

--- a/solution.py
+++ b/solution.py
@@ -22,9 +22,9 @@
 MESSAGES = CHUNKS + LAG
 
 
-def kernel(field, momenta, counts, accept, out, own, send_up, send_down, from_below, from_above, phi0, phi1, phi2, phi3, mom, moves, sides,
-           done, turned, fields, slab, edges, flag, flags, a_ss, a_rs, c_ss, c_rs, ch_ss, ch_rs, f_ss, f_rs, up_ss, up_rs, down_ss, down_rs, z_ss, z_rs, zm_ss, zm_rs,
-           r_ss, r_rs, d_ss, d_rs, e_ss, e_rs, here):
+def kernel(field, momenta, counts_in, accept_in, out, own, send_up, send_down, from_below, from_above, phi0, phi1, phi2, phi3, mom, moves, sides,
+           done, turned, fields, slab, edges, flag, flags, a_ss, a_rs, c_ss, c_rs, ch_ss, ch_rs, f_ss, f_rs, up_ss, down_ss, m_rs, z_ss, z_rs, zm_ss, zm_rs,
+           r_ss, r_rs, d_ss, d_rs, e_ss, e_rs, here, counts, accept):
     rep, gz = lax.axis_index("rep"), lax.axis_index("gz")
     y, z = rep // 4, gz // 2
     q = (gz % 2) * 4 + rep % 4
@@ -50,6 +50,9 @@
     def took(like, sem):
         pltpu.make_async_copy(like, like, sem).wait()
 
+    small = (pltpu.make_async_copy(counts_in, counts, here.at[2]), pltpu.make_async_copy(accept_in, accept, here.at[3]))
+    for copy in small:
+        copy.start()
     for n, (src, dst) in enumerate(((field, fields), (momenta, slab))):
         for side in range(2):
             pltpu.make_async_copy(src.at[0, :, :, pl.ds(side * LANES, LANES)], dst.at[:, side], here.at[n]).start()
@@ -72,6 +75,14 @@
         if step == 0:
             return pltpu.make_async_copy(src, dst, a_rs.at[pair])
         return remote(src, dst, a_ss, a_rs.at[pair], ring(step))
+
+    def first_copy(part, step):
+        start = ((q + step) % 8) * ROWS + part * 16
+        src = fields.at[local_plane(0), :, pl.ds(pl.multiple_of(start, 16), 16)]
+        dst = own.at[0, half, slot, :, pl.ds(part * 16, 16)]
+        if step == 0:
+            return pltpu.make_async_copy(src, dst, a_rs.at[4 * part])
+        return remote(src, dst, a_ss, a_rs.at[4 * part], ring(step))
 
     def momenta_copy(pair, step):
         src = slab.at[local_plane(pair), :, rows_of((q + step) % 8)]
@@ -102,7 +113,9 @@
 
     took(fields, here.at[0])
     for step in range(8):
-        field_copy(0, step).start()
+        first_copy(0, step).start()
+    for copy in small:
+        copy.wait()
     flag[...] = jnp.full(flag.shape, accept[0], jnp.int32)
 
     alive = [[(counts[4 * ((y + d) % 4) + i] > 0).astype(jnp.int32) for i in range(4)] for d in range(4)]
@@ -140,8 +153,9 @@
         return jnp.full((2, 8, LANES), value, jnp.int32) == number
 
     def octet(t):
-        turn = t % 4
-        return t // 4, pl.ds(pl.multiple_of(jnp.where(turn == 0, 0, jnp.where(turn == 1, 24, turn * 8 - 8)), 8), 8)
+        pair, turn = t // 4, t % 4
+        outer = jnp.where(turn == 0, 0, jnp.where(turn == 1, 3, turn - 1))
+        return pair, pl.ds(pl.multiple_of(jnp.where(pair == 0, turn, outer) * 8, 8), 8)
 
     def assemble(t, forward):
         pair, rows = octet(jnp.minimum(t, CHUNKS - 1))
@@ -166,10 +180,10 @@
                 send_up[t, c, h] = up
 
     def up_copy(t):
-        return remote(send_up.at[t], from_below.at[t], up_ss, up_rs.at[t], above)
+        return remote(send_up.at[t], from_below.at[t], up_ss, m_rs.at[t], above)
 
     def down_copy(t):
-        return remote(send_down.at[t], from_above.at[t], down_ss, down_rs.at[t], below)
+        return remote(send_down.at[t], from_above.at[t], down_ss, m_rs.at[t], below)
 
     def pick(u):
         pair, rows = octet(u)
@@ -209,19 +223,27 @@
     row_halo = phi0.at[:, pl.ds(4, 2), :, beside_inner]
 
     def tick(t, carry):
-        @pl.when(t < 3)
+        @pl.when(t == 0)
         def _():
             for step in range(8):
-                field_copy(t + 1, step).start()
-
-        @pl.when((t % 4 == 0) & (t < CHUNKS))
+                first_copy(1, step).start()
+
+        @pl.when((t < 5) & (t % 2 == 0))
+        def _():
+            for step in range(8):
+                field_copy(t // 2 + 1, step).start()
+
+        @pl.when((t == 0) | (t == 2))
+        def _():
+            took(own.at[0, :, :, :, pl.ds(0, 16)], a_rs.at[2 * t])
+
+        @pl.when((t % 4 == 0) & (t > 0) & (t < CHUNKS))
         def _():
             took(own.at[t // 4], a_rs.at[t // 4])
 
         @pl.when(t >= LAG)
         def _():
-            up_copy(t - LAG).wait_recv()
-            down_copy(t - LAG).wait_recv()
+            took(own.at[0, 0], m_rs.at[t - LAG])
 
         @pl.when(t < LAG)
         def _():
@@ -236,7 +258,7 @@
             up_copy(t).start()
             down_copy(t).start()
 
-        @pl.when(t == 4)
+        @pl.when(t == 6)
         def _():
             took(slab, here.at[1])
             fill_edges()
@@ -244,28 +266,28 @@
                 edge_copy(step).start()
                 flag_copy(step).start()
 
-        @pl.when((t >= 6) & (t < 14) & (t % 2 == 0))
+        @pl.when((t >= 8) & (t < 16) & (t % 2 == 0))
         def _():
             for step in range(8):
-                momenta_copy((t - 6) // 2, step).start()
+                momenta_copy((t - 8) // 2, step).start()
 
         @pl.when(t >= 2 * LAG)
         def _():
             pick(t - 2 * LAG)
 
-        @pl.when((t >= 2 * LAG + 1) & ((t - 2 * LAG) % 4 == 1))
+        @pl.when((t == 2 * LAG + 3) | (t == 2 * LAG + 5) | (t == 2 * LAG + 9) | (t == 2 * LAG + 13))
         def _():
             for copy in row_copies((t - 2 * LAG - 1) // 4):
                 copy.start()
 
-        @pl.when((t == 2 * LAG + 3) | (t == 2 * LAG + 7))
-        def _():
-            pair = (t - 2 * LAG - 3) // 4
+        @pl.when((t == 2 * LAG + 5) | (t == 2 * LAG + 7))
+        def _():
+            pair = (t - 2 * LAG - 5) // 2
             took(row_halo, r_rs.at[pair])
             for copy in z_copies(pair):
                 copy.start()
 
-        @pl.when(t == 12)
+        @pl.when(t == 14)
         def _():
             took(mom.at[:, pl.ds(4, 8), :, beside_inner], ch_rs)
             took(momenta_pair, c_rs.at[0])
@@ -453,8 +475,8 @@
         in_specs=[
             pl.BlockSpec(memory_space=pltpu.HBM),
             pl.BlockSpec(memory_space=pltpu.HBM),
-            pl.BlockSpec(memory_space=pltpu.SMEM),
-            pl.BlockSpec(memory_space=pltpu.SMEM),
+            pl.BlockSpec(memory_space=pl.ANY),
+            pl.BlockSpec(memory_space=pl.ANY),
         ],
         out_specs=pl.BlockSpec(memory_space=pltpu.VMEM),
         scratch_shapes=[
@@ -477,10 +499,12 @@
             pltpu.VMEM((8, 4, 2, 8, LANES), f32),
             pltpu.VMEM((8, LANES), jnp.int32),
             pltpu.VMEM((8, 8, LANES), jnp.int32),
-            dma, dma((PAIRS,)), dma, dma((PAIRS,)), dma, dma, dma, dma,
-            dma, dma((MESSAGES,)), dma, dma((MESSAGES,)),
+            dma, dma((PAIRS + 1,)), dma, dma((PAIRS,)), dma, dma, dma, dma,
+            dma, dma, dma((MESSAGES,)),
             dma, dma((2,)), dma, dma,
-            dma, dma((PAIRS,)), dma, dma((2, SLOTS)), dma, dma, dma((2,)),
+            dma, dma((PAIRS,)), dma, dma((2, SLOTS)), dma, dma, dma((4,)),
+            pltpu.SMEM((16,), jnp.int32),
+            pltpu.SMEM((1,), jnp.int32),
         ],
         compiler_params=pltpu.CompilerParams(collective_id=0, has_side_effects=True, vmem_limit_bytes=52 * 1024 * 1024),
     )(field, momenta, counts, accept)

time: 63.5 us -> 61.3 us (0.965)
  Pallas kernels: 61.8 us -> 59.6 us
    pallas_call x1, Pallas kernels: 61.8 us -> 59.6 us  [local(): pl.pallas_call(kernel, out_shape=jax.ShapeDtypeStruct(field.shape, f32),...]
where the time goes in v6:
time: 61.3 us; the launch traced here: 61.2 us
  Pallas kernels  59.6 us (97%)
  local copies, waits for them, and re-layouts  0.98 us (2%)
  between operations  0.68 us (1%)
    pallas_call x1, Pallas kernels, local(): pl.pallas_call(kernel, out_shape=jax.ShapeDtypeStruct(field.shape, f32),...  59.6 us

profile of v6, /device:TPU:1, one launch (start us, length us, event | category | flops | bytes accessed | tf_op | source)
XLA Modules:
  0.0 61.2 jit_solution(2500942320090993109)
XLA Ops:
  0.0 0.0 copy-start
  0.7 0.0 copy-done
  0.7 59.6 %shard_map.46 = f32[1,4,256,256]{3,2,1,0:T(8,128)S(1)} custom-call(f32[1,4,256,256]{3,2,1,0:T(8,128)} %field.1, f32[1,4,256,256]{3,2,1,0:T(8,128)} %momenta.1, s32[16]{0:T(128)S(1)} %copy-done, s32[1]{0:T(128)S(6)} %copy.6.accept_in), custom_call_target="tpu_custom_call" | custom-call | tf_op jit(solution)/shard_map/pallas_call | solution.py:472
  60.3 1.0 %copy.7 = f32[1,4,256,256]{3,2,1,0:T(8,128)} copy(f32[1,4,256,256]{3,2,1,0:T(8,128)S(1)} %shard_map.46) | data formatting | bytes 2097152
Async XLA Ops:
  0.0 0.7 %copy-start = (s32[16]{0:T(128)S(1)}, s32[16]{0:T(128)}, u32[]{:S(2)}) copy-start(s32[16]{0:T(128)} %counts_in.1) | copy-start | bytes 196

commit v7 on v6

--- a/solution.py
+++ b/solution.py
@@ -153,9 +153,11 @@
         return jnp.full((2, 8, LANES), value, jnp.int32) == number
 
     def octet(t):
-        pair, turn = t // 4, t % 4
-        outer = jnp.where(turn == 0, 0, jnp.where(turn == 1, 3, turn - 1))
-        return pair, pl.ds(pl.multiple_of(jnp.where(pair == 0, turn, outer) * 8, 8), 8)
+        turn, late = t % 4, t >= 8
+        pair = jnp.where(late, 2 + t // 2 % 2, t // 4)
+        outer = jnp.where(late, t < 12, turn < 2)
+        piece = jnp.where(outer, t % 2 * 3, 1 + t % 2)
+        return pair, pl.ds(pl.multiple_of(jnp.where(pair == 0, turn, piece) * 8, 8), 8)
 
     def assemble(t, forward):
         pair, rows = octet(jnp.minimum(t, CHUNKS - 1))
@@ -237,9 +239,10 @@
         def _():
             took(own.at[0, :, :, :, pl.ds(0, 16)], a_rs.at[2 * t])
 
-        @pl.when((t % 4 == 0) & (t > 0) & (t < CHUNKS))
-        def _():
-            took(own.at[t // 4], a_rs.at[t // 4])
+        @pl.when((t == 4) | (t == 8) | (t == 10))
+        def _():
+            pair = t // 4 + t // 10
+            took(own.at[pair], a_rs.at[pair])
 
         @pl.when(t >= LAG)
         def _():
@@ -275,9 +278,9 @@
         def _():
             pick(t - 2 * LAG)
 
-        @pl.when((t == 2 * LAG + 3) | (t == 2 * LAG + 5) | (t == 2 * LAG + 9) | (t == 2 * LAG + 13))
-        def _():
-            for copy in row_copies((t - 2 * LAG - 1) // 4):
+        @pl.when((t == 2 * LAG + 3) | (t == 2 * LAG + 5) | (t == 2 * LAG + 9) | (t == 2 * LAG + 11))
+        def _():
+            for copy in row_copies((t - 2 * LAG - 1) // 3):
                 copy.start()
 
         @pl.when((t == 2 * LAG + 5) | (t == 2 * LAG + 7))

time: 61.3 us -> 61.2 us (level)
  no operation moved by 1% of the time
where the time goes in v7:
time: 61.2 us; the launch traced here: 61.1 us
  Pallas kernels  59.4 us (97%)
  local copies, waits for them, and re-layouts  0.98 us (2%)
  between operations  0.68 us (1%)
    pallas_call x1, Pallas kernels, local(): pl.pallas_call(kernel, out_shape=jax.ShapeDtypeStruct(field.shape, f32),...  59.4 us

profile of v7, /device:TPU:1, one launch (start us, length us, event | category | flops | bytes accessed | tf_op | source)
XLA Modules:
  0.0 61.1 jit_solution(11910800145294275801)
XLA Ops:
  0.0 0.0 copy-start
  0.7 0.0 copy-done
  0.7 59.4 %shard_map.46 = f32[1,4,256,256]{3,2,1,0:T(8,128)S(1)} custom-call(f32[1,4,256,256]{3,2,1,0:T(8,128)} %field.1, f32[1,4,256,256]{3,2,1,0:T(8,128)} %momenta.1, s32[16]{0:T(128)S(1)} %copy-done, s32[1]{0:T(128)S(6)} %copy.6.accept_in), custom_call_target="tpu_custom_call" | custom-call | tf_op jit(solution)/shard_map/pallas_call | solution.py:475
  60.1 1.0 %copy.7 = f32[1,4,256,256]{3,2,1,0:T(8,128)} copy(f32[1,4,256,256]{3,2,1,0:T(8,128)S(1)} %shard_map.46) | data formatting | bytes 2097152
Async XLA Ops:
  0.0 0.7 %copy-start = (s32[16]{0:T(128)S(1)}, s32[16]{0:T(128)}, u32[]{:S(2)}) copy-start(s32[16]{0:T(128)} %counts_in.1) | copy-start | bytes 196

commit v8 on v7

--- a/solution.py
+++ b/solution.py
@@ -389,10 +389,9 @@
         move = each(lambda m, f: m + f, move, push)
         return move, each(lambda c, m: c + m, trio[1], move)
 
-    def one_slot(n, carry):
+    def opening(n, carry):
         s = (n % 2) * 2 + n // 2
-        taken = flags[s] == 1
-        start, second, third, held = phi0.at[s], phi2.at[s], phi3.at[s], moves.at[s]
+        start, second, held = phi0.at[s], phi2.at[s], moves.at[s]
         trio = [None, natural(start, 2), natural(start, 3)]
         for plane in range(3, 13):
             trio = trio[1:] + [natural(start, plane + 1)]
@@ -409,6 +408,12 @@
             keep(second, plane, value)
         for copy in end_copies(2, s):
             copy.start()
+        return carry
+
+    def inner_planes(n, carry):
+        s = (n % 2) * 2 + n // 2
+        taken = flags[s] == 1
+        second, third, held = phi2.at[s], phi3.at[s], moves.at[s]
         trio = [None, packed(second, 0), packed(second, 1)]
         for plane in range(1, 7):
             trio = trio[1:] + [packed(second, plane + 1)]
@@ -450,7 +455,9 @@
         results(s, 2)
         return carry
 
-    lax.fori_loop(0, SLOTS, one_slot, 0)
+    for some in ((0, 1), (1, SLOTS)):
+        lax.fori_loop(*some, opening, 0)
+        lax.fori_loop(*some, inner_planes, 0)
     lax.fori_loop(0, SLOTS, next_planes, 0)
     lax.fori_loop(0, SLOTS, end_planes, 0)
 

time: 61.2 us -> 61.5 us (level)
  no operation moved by 1% of the time
where the time goes in v8:
time: 61.5 us; the launch traced here: 61.4 us
  Pallas kernels  59.7 us (97%)
  local copies, waits for them, and re-layouts  0.98 us (2%)
  between operations  0.68 us (1%)
    pallas_call x1, Pallas kernels, local(): pl.pallas_call(kernel, out_shape=jax.ShapeDtypeStruct(field.shape, f32),...  59.7 us

profile of v8, /device:TPU:1, one launch (start us, length us, event | category | flops | bytes accessed | tf_op | source)
XLA Modules:
  0.0 61.4 jit_solution(14434595152364018913)
XLA Ops:
  0.0 0.0 copy-start
  0.7 0.0 copy-done
  0.7 59.7 %shard_map.46 = f32[1,4,256,256]{3,2,1,0:T(8,128)S(1)} custom-call(f32[1,4,256,256]{3,2,1,0:T(8,128)} %field.1, f32[1,4,256,256]{3,2,1,0:T(8,128)} %momenta.1, s32[16]{0:T(128)S(1)} %copy-done, s32[1]{0:T(128)S(6)} %copy.6.accept_in), custom_call_target="tpu_custom_call" | custom-call | tf_op jit(solution)/shard_map/pallas_call | solution.py:482
  60.4 1.0 %copy.7 = f32[1,4,256,256]{3,2,1,0:T(8,128)} copy(f32[1,4,256,256]{3,2,1,0:T(8,128)S(1)} %shard_map.46) | data formatting | bytes 2097152
Async XLA Ops:
  0.0 0.7 %copy-start = (s32[16]{0:T(128)S(1)}, s32[16]{0:T(128)}, u32[]{:S(2)}) copy-start(s32[16]{0:T(128)} %counts_in.1) | copy-start | bytes 196

commit v9 on v7

--- a/solution.py
+++ b/solution.py
@@ -230,10 +230,10 @@
             for step in range(8):
                 first_copy(1, step).start()
 
-        @pl.when((t < 5) & (t % 2 == 0))
+        @pl.when((t == 1) | (t == 2) | (t == 4))
         def _():
             for step in range(8):
-                field_copy(t // 2 + 1, step).start()
+                field_copy((t + 2) // 2, step).start()
 
         @pl.when((t == 0) | (t == 2))
         def _():

time: 61.2 us -> 61 us (level)
  no operation moved by 1% of the time
where the time goes in v9:
time: 61 us; the launch traced here: 60.9 us
  Pallas kernels  59.2 us (97%)
  local copies, waits for them, and re-layouts  0.98 us (2%)
  between operations  0.68 us (1%)
    pallas_call x1, Pallas kernels, local(): pl.pallas_call(kernel, out_shape=jax.ShapeDtypeStruct(field.shape, f32),...  59.2 us

profile of v9, /device:TPU:1, one launch (start us, length us, event | category | flops | bytes accessed | tf_op | source)
XLA Modules:
  0.0 60.9 jit_solution(3887838471829675567)
XLA Ops:
  0.0 0.0 copy-start
  0.7 0.0 copy-done
  0.7 59.2 %shard_map.46 = f32[1,4,256,256]{3,2,1,0:T(8,128)S(1)} custom-call(f32[1,4,256,256]{3,2,1,0:T(8,128)} %field.1, f32[1,4,256,256]{3,2,1,0:T(8,128)} %momenta.1, s32[16]{0:T(128)S(1)} %copy-done, s32[1]{0:T(128)S(6)} %copy.6.accept_in), custom_call_target="tpu_custom_call" | custom-call | tf_op jit(solution)/shard_map/pallas_call | solution.py:475
  59.9 1.0 %copy.7 = f32[1,4,256,256]{3,2,1,0:T(8,128)} copy(f32[1,4,256,256]{3,2,1,0:T(8,128)S(1)} %shard_map.46) | data formatting | bytes 2097152
Async XLA Ops:
  0.0 0.7 %copy-start = (s32[16]{0:T(128)S(1)}, s32[16]{0:T(128)}, u32[]{:S(2)}) copy-start(s32[16]{0:T(128)} %counts_in.1) | copy-start | bytes 196
